TPU v7x, 512 devices: a whole 4x8x8 slice. The times are simulated.
512 devices in a mesh: node: 64 (over z, x, core), feat: 8 (over y).
Axes of the slice: x: 4, y: 8, z: 8, core: 2. Of those that a mesh axis runs over, the one named last changes fastest.
Arguments:
- features: bfloat16 [262144, 512], P('node', 'feat'), may hold values from -6 to 6
- weight: bfloat16 [512, 512], P('feat'), may hold values from -0.25 to 0.25
- tile_row: int32 [5120], P('node'), may hold values from 0 to 31
- tile_col: int32 [5120], P('node'), may hold values from 0 to 95
- tile_count: int32 [64], P('node'), may hold values from 40 to 80, as said below
- send_blocks: int32 [64, 64, 1], P('node'), may hold values from 0 to 31
- tile_values: bfloat16 [5120, 128, 128], P('node'), may hold values from -0.3125 to 0.3125
- upstream: bfloat16 [262144, 512], P('node', 'feat'), may hold values from -6 to 6
Outputs:
- features_grad: bfloat16 [262144, 512], P('node', 'feat')
- weight_grad: float32 [512, 512], P('feat')
Inputs may be any that keep to these rules, and one draw needn't show every extreme that they name: `tile_count`: every partition has 40 or more live tiles, and one partition has exactly 80. Sixteen of the live tiles of each partition q are tiles that read the received slots of the 16 partitions (q + d) mod 64 for d in ±1, ±2, …, ±7, +8 and +32, one tile each; every other tile reads one of the partition's own blocks.
All inputs are finite; a program needn't handle non-finite values.
Results may differ from a plain program's by a relative error of at most 0.0061.
Values may be sent and summed in bfloat16 or wider, within the bound.
A program may use at most 64 MiB of HBM per device.

v0:
```python
import math

import jax
import jax.numpy as jnp
from jax import lax
from jax.sharding import PartitionSpec as P

BLK = 128


def silu_slope(pre_act):
    sig = jax.nn.sigmoid(pre_act)
    return sig * (1.0 + pre_act * (1.0 - sig))


def local(features, weight, tile_row, tile_col, tile_count, send_blocks, tile_values, upstream):
    rows_dev, width = features.shape
    block_count = rows_dev // BLK
    node_count = lax.axis_size("node")
    slot_count = send_blocks.shape[2]
    my_sends = send_blocks[0]
    blocked = features.reshape(block_count, BLK, width)
    arrived = lax.all_to_all(blocked[my_sends], "node", split_axis=0, concat_axis=0, tiled=True)
    table = jnp.concatenate([blocked, arrived.reshape(node_count * slot_count, BLK, width)], 0)
    live_count = tile_count[0]
    per_turn = 16
    num_turns = (live_count + per_turn - 1) // per_turn

    def tile_slice(turn):
        offset = turn * per_turn
        row_ids = lax.dynamic_slice_in_dim(tile_row, offset, per_turn)
        col_ids = lax.dynamic_slice_in_dim(tile_col, offset, per_turn)
        tile_vals = lax.dynamic_slice_in_dim(tile_values, offset, per_turn, 0)
        alive = (offset + jnp.arange(per_turn) < live_count).astype(jnp.float32)
        return (row_ids, col_ids, tile_vals, alive)

    def forward_turn(turn, totals):
        row_ids, col_ids, tile_vals, alive = tile_slice(turn)
        sources = table[col_ids]
        terms = jnp.einsum("tij,tjf->tif", tile_vals, sources, preferred_element_type=jnp.float32)
        return totals.at[row_ids].add(terms * alive[:, None, None])

    start_totals = jnp.zeros((block_count, BLK, width), jnp.float32)
    totals = lax.fori_loop(0, num_turns, forward_turn, start_totals)
    aggregated = totals.reshape(rows_dev, width).astype(jnp.bfloat16)
    weights = lax.all_gather(weight, "feat", axis=0, tiled=True)
    column_start = lax.axis_index("feat") * width
    weight_cols = lax.dynamic_slice_in_dim(weights, column_start, width, 1)
    weight_mine = lax.dynamic_slice_in_dim(weights, column_start, width, 0)
    pre_act = jnp.dot(
        lax.all_gather(aggregated, "feat", axis=1, tiled=True),
        weight_cols,
        preferred_element_type=jnp.float32,
    )
    grad_pre = (upstream.astype(jnp.float32) * silu_slope(pre_act)).astype(jnp.bfloat16)
    shard_piece = lax.all_gather(grad_pre, "feat", axis=1, tiled=True)
    block_grad = jnp.einsum(
        "nf,ng->fg", aggregated, shard_piece, preferred_element_type=jnp.float32
    )
    grad_rows = block_grad
    grad_sum = jnp.einsum("ng,fg->nf", shard_piece, weight_mine, preferred_element_type=jnp.float32)
    grad_rows, grad_sum = (grad_rows, grad_sum)
    grad_agg = grad_sum.astype(jnp.bfloat16)
    weight_grad = lax.psum(grad_rows, "node")
    weight_grad = weight_grad / math.sqrt(rows_dev * node_count)
    grad_blocks = grad_agg.reshape(block_count, BLK, width)

    def backward_turn(turn, scattered):
        row_ids, col_ids, tile_vals, alive = tile_slice(turn)
        sources = grad_blocks[row_ids]
        terms = jnp.einsum("tji,tjf->tif", tile_vals, sources, preferred_element_type=jnp.float32)
        return scattered.at[col_ids].add(terms * alive[:, None, None])

    start_scattered = jnp.zeros((block_count + node_count * slot_count, BLK, width), jnp.float32)
    scattered = lax.fori_loop(0, num_turns, backward_turn, start_scattered)
    outgoing = scattered[block_count:].reshape(node_count, slot_count, BLK, width)
    returned = lax.all_to_all(outgoing, "node", split_axis=0, concat_axis=0, tiled=True)
    grad_feat = (
        scattered[:block_count]
        .at[my_sends.reshape(-1)]
        .add(returned.reshape(node_count * slot_count, BLK, width))
    )
    features_grad = grad_feat.reshape(rows_dev, width).astype(jnp.bfloat16)
    return (features_grad, weight_grad)


def solution(mesh):
    in_specs = (
        P("node", "feat"),
        P("feat", None),
        P("node"),
        P("node"),
        P("node"),
        P("node", None, None),
        P("node", None, None),
        P("node", "feat"),
    )
    out_specs = (P("node", "feat"), P("feat", None))
    return jax.shard_map(local, mesh=mesh, in_specs=in_specs, out_specs=out_specs, check_vma=False)
```

profile of v0, /device:TPU:1, one launch (start us, length us, event | category | flops | bytes accessed | tf_op | source)
XLA Modules:
  0.0 471.2 jit_solution(5932481758247486306)
XLA Ops:
  8.4 1.7 gather_fusion.2
  10.0 14.8 %all-to-all-start = ((bf16[64,1,128,64]{2,3,1,0:T(8,128)(2,1)}), bf16[64,1,128,64]{2,3,1,0:T(8,128)(2,1)S(1)}, u32[]{:S(2)}, u32[]{:S(2)}) async-start(bf16[64,1,128,64]{2,3,1,0:T(8,128)(2,1)} %bitcast.4), calls=%async_computation | async-start | bytes 2097152 | tf_op jit(solution)/shard_map/all_to_all | solution.py:23
  25.6 27.3 %all-to-all-done = bf16[64,1,128,64]{2,3,1,0:T(8,128)(2,1)S(1)} async-done(((bf16[64,1,128,64]{2,3,1,0:T(8,128)(2,1)}), bf16[64,1,128,64]{2,3,1,0:T(8,128)(2,1)S(1)}, u32[]{:S(2)}, u32[]{:S(2)}) %all-to-all-start) | async-done | bytes 1048608 | tf_op jit(solution)/shard_map/all_to_all | solution.py:23
  53.8 1.4 pad_maximum_fusion
  55.2 2.7 copy.39
  58.1 31.0 %while.20 = (s32[]{:T(128)}, f32[32,128,64]{1,2,0:T(8,128)S(1)}, s32[]{:T(128)}, s32[80]{0:T(128)S(1)}, bf16[80,128,128]{2,1,0:T(8,128)(2,1)}, /*index=5*/s32[80...) while((s32[]{:T(128)}, f32[32,128,64]{1,2,0:T(8,128)S(1)}, ...), condition=%wide.region_2.3_spmd, body=%wide.region_0.2_spmd.sunk | while | flops 33817748 | bytes 3412723 | solution.py:44
  58.9 2.5 gather_fusion
  61.4 1.5 convolution_multiply_fusion.4
  63.0 1.3 scatter_fusion
  65.1 2.5 gather_fusion
  67.6 1.5 convolution_multiply_fusion.4
  71.3 2.5 gather_fusion
  73.8 1.5 convolution_multiply_fusion.4
  75.3 1.3 scatter_fusion
  77.5 2.5 gather_fusion
  80.0 1.5 convolution_multiply_fusion.4
  83.6 2.5 gather_fusion
  86.2 1.5 convolution_multiply_fusion.4
  87.7 1.3 scatter_fusion
  90.0 23.0 %all_gather.10 = bf16[512,512]{1,0:T(8,128)(2,1)S(1)} all-gather(bf16[64,512]{1,0:T(8,128)(2,1)S(1)} %copy-done.2), channel_id=1, replica_groups=mesh['node'=64,'feat'=8] {'feat'}, dimensions={0}, use_global_device_ids=true | all-gather | bytes 589824 | tf_op jit(solution)/shard_map/all_gather | solution.py:46
  113.0 34.3 %all-gather.3.cloned.1.call-done = bf16[4096,512]{0,1:T(8,128)(2,1)} async-done(((bf16[4096,64]{0,1:T(8,128)(2,1)}), bf16[4096,512]{0,1:T(8,128)(2,1)}) %all-gather.3.cloned.1.call-update) | async-done | bytes 4194320 | tf_op jit(solution)/shard_map/all_gather | solution.py:51
  147.3 4.3 multiply_convert_fusion
  151.6 54.8 %all-gather.5.cloned.1.call-done = bf16[4096,512]{0,1:T(8,128)(2,1)} async-done(((bf16[4096,64]{0,1:T(8,128)(2,1)}), bf16[4096,512]{0,1:T(8,128)(2,1)}) %all-gather.5.cloned.1.call-update) | async-done | bytes 4194320 | tf_op jit(solution)/shard_map/all_gather | solution.py:56
  206.4 3.0 convolution_convert_fusion
  209.4 1.4 copy.45
  210.8 2.1 broadcast_in_dim.22
  212.8 33.3 %while.21 = (s32[]{:T(128)}, f32[96,128,64]{1,2,0:T(8,128)}, s32[]{:T(128)}, s32[80]{0:T(128)S(1)}, bf16[80,128,128]{2,1,0:T(8,128)(2,1)}, /*index=5*/s32[80]{0:...) while((s32[]{:T(128)}, f32[96,128,64]{1,2,0:T(8,128)}, ...), condition=%wide.region_5.6_spmd, body=%wide.region_3.5_spmd.sunk | while | flops 33817748 | bytes 3412723 | solution.py:75
  213.6 1.9 gather_fusion.1
  215.5 1.4 convolution_multiply_fusion.5
  216.8 2.7 scatter_fusion.1
  220.2 1.9 gather_fusion.1
  222.1 1.4 convolution_multiply_fusion.5
  223.5 2.7 scatter_fusion.1
  226.9 1.9 gather_fusion.1
  228.8 1.4 convolution_multiply_fusion.5
  230.2 2.7 scatter_fusion.1
  233.6 1.9 gather_fusion.1
  235.5 1.4 convolution_multiply_fusion.5
  236.8 2.7 scatter_fusion.1
  240.3 1.9 gather_fusion.1
  242.1 1.4 convolution_multiply_fusion.5
  243.5 2.7 scatter_fusion.1
  246.2 3.1 slice_bitcast_fusion
  249.3 11.2 %all-to-all-start.1 = ((f32[64,1,128,64]{2,3,1,0:T(8,128)}), f32[64,1,128,64]{2,3,1,0:T(8,128)}, u32[]{:S(2)}, u32[]{:S(2)}) async-start(f32[64,1,128,64]{2,3,1,0:T(8,128)} %slice_bitcast_fusion), calls=%async_computation.1 | async-start | bytes 4194304 | tf_op jit(solution)/shard_map/all_to_all | solution.py:77
  260.6 4.2 fusion.13
  266.2 189.0 %all-reduce.2.cloned.1.call-done = f32[64,512]{1,0:T(8,128)} async-done(((f32[64,512]{1,0:T(8,128)}), f32[64,512]{1,0:T(8,128)}) %all-reduce.2.cloned.1.call-update) | async-done | bytes 131088 | tf_op jit(solution)/shard_map/psum | solution.py:64
  455.2 1.6 broadcast_multiply_fusion
  456.8 7.0 %scatter_fusion.2 = f32[32,128,64]{1,2,0:T(8,128)S(1)} fusion(f32[32,128,64]{1,2,0:T(8,128)S(1)} %slice.6, s32[64]{0:T(128)S(1)} %fusion.10, f32[64,128,64]{1,2,0:T(8,128)} %bitcast.10), kind=kCustom, calls=%fused_computation.5 | custom fusion | flops 524288 | bytes 6291712 | tf_op jit(solution)/shard_map/scatter-add | solution.py:81
  (59 shorter events, 15.5 us)
Async XLA Ops:
  7.2 1.1 copy-start
  10.0 42.8 %all-to-all-start = ((bf16[64,1,128,64]{2,3,1,0:T(8,128)(2,1)}), bf16[64,1,128,64]{2,3,1,0:T(8,128)(2,1)S(1)}, u32[]{:S(2)}, u32[]{:S(2)}) async-start(bf16[64,1,128,64]{2,3,1,0:T(8,128)(2,1)} %bitcast.4), calls=%async_computation | async-start | bytes 2097152 | tf_op jit(solution)/shard_map/all_to_all | solution.py:23
  24.9 122.5 %all-gather.3.cloned.1.call-start = ((), (), s32[]{:S(2)}) async-start(), calls=%async_computation.2 | async-start | bytes 4718592 | tf_op jit(solution)/shard_map/all_gather | solution.py:51
  52.9 1.0 copy-start.1
  55.2 2.9 copy-start.3
  55.2 2.9 copy-start.4
  58.1 31.9 %copy-start.2 = (bf16[64,512]{1,0:T(8,128)(2,1)S(1)}, bf16[64,512]{1,0:T(8,128)(2,1)}, u32[]{:S(2)}) copy-start(bf16[64,512]{1,0:T(8,128)(2,1)} %param.13) | copy-start | bytes 196612
  90.0 116.4 %all-gather.5.cloned.1.call-start = ((), (), s32[]{:S(2)}) async-start(), calls=%async_computation.3 | async-start | bytes 4718592 | tf_op jit(solution)/shard_map/all_gather | solution.py:56
  249.3 207.5 %all-to-all-start.1 = ((f32[64,1,128,64]{2,3,1,0:T(8,128)}), f32[64,1,128,64]{2,3,1,0:T(8,128)}, u32[]{:S(2)}, u32[]{:S(2)}) async-start(f32[64,1,128,64]{2,3,1,0:T(8,128)} %slice_bitcast_fusion), calls=%async_computation.1 | async-start | bytes 4194304 | tf_op jit(solution)/shard_map/all_to_all | solution.py:77
  260.5 4.3 copy-start.5
  260.5 194.7 %all-reduce.2.cloned.1.call-start = ((), (), s32[]{:S(2)}) async-start(), calls=%async_computation.4 | async-start | bytes 262144 | tf_op jit(solution)/shard_map/psum | solution.py:64
Sparse Core Ops, SparseCore 0:
  90.1 57.1 all-gather.2
  151.7 54.6 all-gather.4
  265.4 189.7 all-reduce.1
where the time goes:
time: 473 us; the launch traced here: 471 us
  waiting for transfers between devices  305 us (64%)
  other arithmetic  39.8 us (8%)
  local copies, waits for them, and re-layouts  35.9 us (8%)
  starting transfers between devices  26.2 us (6%)
  matrix products  26 us (5%)
  blocking collectives  23 us (5%)
  between operations  14.6 us (3%)
    psum x1, waiting for transfers between devices, local(): weight_grad = lax.psum(grad_rows, 'node')  189 us
    all_gather x1, waiting for transfers between devices, local(): shard_piece = lax.all_gather(grad_pre, 'feat', axis=1, tiled=True)  54.8 us
    all_gather x1, waiting for transfers between devices, local(): lax.all_gather(aggregated, 'feat', axis=1, tiled=True)  34.3 us
    all_to_all x1, waiting for transfers between devices, local(): lax.all_to_all(blocked[my_sends], 'node', split_axis=0, concat_axis=0, ti...  27.3 us
    all_gather x1, blocking collectives, local(): weights = lax.all_gather(weight, 'feat', axis=0, tiled=True)  23 us
    all_to_all x1, starting transfers between devices, local(): lax.all_to_all(blocked[my_sends], 'node', split_axis=0, concat_axis=0, ti...  14.8 us
    scatter-add x5, other arithmetic, backward_turn(): return scattered.at[col_ids].add(terms * alive[:, None, None])  13.4 us
    gather x5, local copies, waits for them, and re-layouts, forward_turn(): sources = table[col_ids]  12.7 us
  transfers between devices with their start and end apart: 5, of which 4 were waited for; matrix products, arithmetic and copies ran while one was open for 2% of the time, Pallas kernels for 0%

commit v1 on v0

v1 whole, which is shorter than its diff:
```python
import functools
import math

import jax
import jax.numpy as jnp
from jax import lax
from jax.experimental import pallas as pl
from jax.experimental.pallas import tpu as pltpu
from jax.sharding import PartitionSpec as P

MESH = pl.DeviceIdType.MESH
F32 = jnp.float32
BF16 = jnp.bfloat16
BLK = 128
CORES = 2
X_CHIPS = 4


def halo_offsets(node_count):
    near = [step for d in range(1, 8) for step in (d, -d)]
    return near + [8, 32]


class Plan:
    def __init__(self, blocks, width, tiles, feats, nodes, offsets, x_chips):
        self.blocks, self.width, self.tiles = blocks, width, tiles
        self.feats, self.nodes, self.offsets = feats, nodes, offsets
        self.halo = len(offsets)
        self.local = tiles - self.halo
        self.full = width * feats
        self.stages = blocks // (2 * feats)
        self.xs = x_chips
        self.zs = nodes // (CORES * x_chips)
        at = 0
        for name, size in (
            ("fl_t", self.local), ("fl_c", self.local), ("fl_k", self.local), ("fl_end", blocks),
            ("fh_t", self.halo), ("fh_s", self.halo), ("fh_k", self.halo), ("fh_end", blocks),
            ("bh_t", self.halo), ("bh_r", self.halo),
            ("bl_t", self.local), ("bl_r", self.local), ("bl_k", self.local), ("bl_end", blocks),
            ("r_s", self.halo), ("r_k", self.halo), ("r_end", blocks),
            ("send", self.halo),
        ):
            setattr(self, name, at)
            at += size
        self.length = at


def ordered(key, payloads, keep):
    rank = jnp.sum((key[None, :] < key[:, None]).astype(jnp.int32), axis=1)
    place = rank[None, :] == jnp.arange(keep, dtype=jnp.int32)[:, None]
    return [jnp.sum(jnp.where(place, p[None, :], 0), axis=1) for p in payloads]


def group_marks(group, count):
    follows = jnp.concatenate([jnp.zeros((1,), jnp.int32), (group[1:] == group[:-1]).astype(jnp.int32)])
    ids = jnp.arange(count, dtype=jnp.int32)[:, None]
    upto = jnp.sum((group[None, :] <= ids).astype(jnp.int32), axis=1)
    some = jnp.any(group[None, :] == ids, axis=1)
    return follows, jnp.where(some, upto, 0)


def index_lists(plan, tile_row, tile_col, tile_count, send_blocks):
    n = plan.nodes
    me = lax.axis_index("node")
    offsets = jnp.array(plan.offsets, jnp.int32)
    t = jnp.arange(plan.tiles, dtype=jnp.int32)
    alive = t < tile_count[0]
    local = alive & (tile_col < plan.blocks)
    read_from = plan.blocks + (me + offsets + n) % n
    is_halo = alive[None, :] & (tile_col[None, :] == read_from[:, None])
    bh_t = jnp.sum(jnp.where(is_halo, t[None, :], 0), axis=1)
    bh_r = jnp.sum(jnp.where(is_halo, tile_row[None, :], 0), axis=1)
    send_to = (me - offsets + n) % n
    sends = send_blocks[0, :, 0]
    nodes = jnp.arange(n, dtype=jnp.int32)
    send = jnp.sum(jnp.where(nodes[None, :] == send_to[:, None], sends[None, :], 0), axis=1)
    slot = jnp.arange(plan.halo, dtype=jnp.int32)

    row_or_none = jnp.where(local, tile_row, plan.blocks)
    col_or_none = jnp.where(local, tile_col, plan.blocks)
    fl_t, fl_r, fl_c = ordered(row_or_none * plan.tiles + t, (t, row_or_none, col_or_none), plan.local)
    fl_k, fl_end = group_marks(fl_r, plan.blocks)
    fh_t, fh_r, fh_s = ordered(bh_r * plan.halo + slot, (bh_t, bh_r, slot), plan.halo)
    fh_k, fh_end = group_marks(fh_r, plan.blocks)
    bl_t, bl_c, bl_r = ordered(col_or_none * plan.tiles + t, (t, col_or_none, row_or_none), plan.local)
    bl_k, bl_end = group_marks(bl_c, plan.blocks)
    r_s, r_c = ordered(send * plan.halo + slot, (slot, send), plan.halo)
    r_k, r_end = group_marks(r_c, plan.blocks)
    return jnp.concatenate(
        [fl_t, fl_c, fl_k, fl_end, fh_t, fh_s, fh_k, fh_end, bh_t, bh_r, bl_t, bl_r, bl_k, bl_end, r_s, r_k, r_end, send]
    )


def kernel(plan, idx, feats_hbm, up_hbm, w_hbm, tiles_hbm, out_ref, wout_ref, s):
    nf, nn, width = plan.feats, plan.nodes, plan.width
    zs, xs = plan.zs, plan.xs
    half = BLK // 2
    node, f = lax.axis_index("node"), lax.axis_index("feat")
    c = lax.rem(node, CORES)
    x = lax.rem(node // CORES, xs)
    z = node // (CORES * xs)

    def node_of(z_at, x_at, c_at):
        return (z_at * xs + x_at) * CORES + c_at

    def remote(src, dst, send_sem, recv_sem, to):
        return pltpu.make_async_remote_copy(
            src_ref=src, dst_ref=dst, send_sem=send_sem, recv_sem=recv_sem, device_id=to, device_id_type=MESH
        )

    get_feats = pltpu.make_async_copy(feats_hbm, s.table.at[pl.ds(0, plan.blocks)], s.get.at[0])
    get_up = pltpu.make_async_copy(up_hbm, s.up, s.get.at[1])
    get_w = pltpu.make_async_copy(w_hbm.at[pl.ds(c * (width // 2), width // 2)], s.wh.at[c, f], s.get.at[2])
    get_tiles = pltpu.make_async_copy(tiles_hbm, s.tiles, s.get.at[3])
    get_feats.start()
    get_up.start()
    get_w.start()
    get_tiles.start()

    near = sorted({d % nn for d in plan.offsets} | {-d % nn for d in plan.offsets})
    partners = [(lax.rem(node + d, nn), f) for d in near]
    partners += [(node, lax.rem(f + d, nf)) for d in range(1, nf)]
    partners += [(node_of(lax.rem(z + d, zs), x, c), f) for d in range(1, zs)]
    plane = [(dx, dc) for dx in range(xs) for dc in range(CORES) if dx or dc]
    partners += [(node_of(z, lax.rem(x + dx, xs), lax.rem(c + dc, CORES)), f) for dx, dc in plane]
    barrier = pltpu.get_barrier_semaphore()
    for to in partners:
        pl.semaphore_signal(barrier, inc=1, device_id=to, device_id_type=MESH)

    get_feats.wait()
    s.table[plan.blocks] = jnp.zeros((BLK, width), BF16)
    for i in range(plan.halo):
        block = s.table[idx[plan.send + i]]
        s.hsend[i] = jnp.concatenate([block[:half], block[half:]], axis=1)
    get_up.wait()

    def pack_up(p, _):
        s.upk[p] = jnp.concatenate([s.up[2 * p], s.up[2 * p + 1]], axis=1)
        return 0

    lax.fori_loop(0, plan.blocks // 2, pack_up, 0)
    for k in range(plan.stages):
        s.ur[k, f] = s.upk[k * nf + f]
    get_w.wait()

    pl.semaphore_wait(barrier, len(partners))

    far_first = sorted(range(1, nf), key=lambda d: -min(d, nf - d))
    halo_copies = []
    for i, d in enumerate(plan.offsets):
        to = (lax.rem(node - d + nn, nn), f)
        halo_copies.append(remote(s.hsend.at[i], s.hrecv.at[i], s.halo_s.at[i], s.halo_r.at[i], to))
    w_copies = [
        remote(s.wh.at[c, f], s.wh.at[c, f], s.w_s.at[d - 1], s.w_r.at[d - 1], (node, lax.rem(f + d, nf)))
        for d in far_first
    ]
    up_copies = []
    for k in range(plan.stages):
        for d in far_first:
            j = lax.rem(f + d, nf)
            up_copies.append(
                remote(s.upk.at[k * nf + j], s.ur.at[k, f], s.up_s.at[k, d - 1], s.up_r.at[k, d - 1], (node, j))
            )
    for copy in halo_copies + w_copies + up_copies:
        copy.start()

    s.fsum[0] = jnp.zeros((BLK, width), F32)
    s.hsum[0] = jnp.zeros((BLK, width), F32)
    get_tiles.wait()

    def forward_local(i, total):
        keep = idx[plan.fl_k + i].astype(F32)
        term = jnp.dot(s.tiles[idx[plan.fl_t + i]], s.table[idx[plan.fl_c + i]], preferred_element_type=F32)
        total = total * keep + term
        s.fsum[i + 1] = total
        return total

    zero = jnp.zeros((BLK, width), F32)
    lax.fori_loop(0, plan.local, forward_local, zero, unroll=8)

    for copy in w_copies:
        copy.wait()
    other = (node_of(z, x, 1 - c), f)
    w_swap = remote(s.wh.at[c], s.wh.at[c], s.wx.at[0], s.wx.at[1], other)
    w_swap.start()

    for copy in halo_copies:
        copy.wait()
    for i in range(plan.halo):
        block = s.hrecv[i]
        s.htable[i] = jnp.concatenate([block[:, :width], block[:, width:]], axis=0)

    def forward_halo(i, total):
        keep = idx[plan.fh_k + i].astype(F32)
        term = jnp.dot(s.tiles[idx[plan.fh_t + i]], s.htable[idx[plan.fh_s + i]], preferred_element_type=F32)
        total = total * keep + term
        s.hsum[i + 1] = total
        return total

    lax.fori_loop(0, plan.halo, forward_halo, zero, unroll=min(8, plan.halo))

    def summed(b):
        return (s.fsum[idx[plan.fl_end + b]] + s.hsum[idx[plan.fh_end + b]]).astype(BF16)

    agg_copies = []
    for k in range(plan.stages):
        stage_copies = []
        for d in far_first + [0]:
            j = lax.rem(f + d, nf)
            p = k * nf + j
            pair = jnp.concatenate([summed(2 * p), summed(2 * p + 1)], axis=1)
            if d == 0:
                s.ar[k, f] = pair
            else:
                s.apk[p] = pair
                copy = remote(s.apk.at[p], s.ar.at[k, f], s.ag_s.at[k, d - 1], s.ag_r.at[k, d - 1], (node, j))
                copy.start()
                stage_copies.append(copy)
        agg_copies.append(stage_copies)

    w_swap.wait()
    for j in range(nf):
        for h in range(CORES):
            rows = width // CORES
            s.wfull[pl.ds(j * width + h * rows, rows)] = s.wh[h, j]

    for copy in up_copies:
        copy.wait()

    def rows_of(ref, k):
        top = jnp.concatenate([ref[k, j][:, :width] for j in range(nf)], axis=1)
        bottom = jnp.concatenate([ref[k, j][:, width:] for j in range(nf)], axis=1)
        return jnp.concatenate([top, bottom], axis=0)

    grad_copies = []
    cols = plan.full // CORES
    for k in range(plan.stages):
        for copy in agg_copies[k]:
            copy.wait()
        s.xrows[...] = rows_of(s.ar, k)
        pre = jnp.dot(s.xrows[...], s.wfull[...], preferred_element_type=F32)
        sig = jax.nn.sigmoid(pre)
        upstream = rows_of(s.ur, k).astype(F32)
        s.gp[...] = (upstream * sig * (1.0 + pre * (1.0 - sig))).astype(BF16)
        grad = lax.dot_general(s.wfull[...], s.gp[...], (((1,), (1,)), ((), ())), preferred_element_type=F32)
        grad = grad.astype(BF16)
        for j in range(nf):
            s.gsend[k, j, 0] = grad[j * width : (j + 1) * width, :BLK]
            s.gsend[k, j, 1] = grad[j * width : (j + 1) * width, BLK:]
        for d in far_first:
            j = lax.rem(f + d, nf)
            copy = remote(
                s.gsend.at[k, j], s.grad.at[pl.ds(2 * (k * nf + f), 2)], s.gr_s.at[k, d - 1], s.gr_r.at[k, d - 1], (node, j)
            )
            copy.start()
            grad_copies.append(copy)
        s.grad[pl.ds(2 * (k * nf + f), 2)] = s.gsend[k, f]
        wg = lax.dot_general(s.xrows[...], s.gp[...], (((0,), (0,)), ((), ())), preferred_element_type=F32)
        for h in range(CORES):
            part = wg[:, h * cols : (h + 1) * cols].reshape(nf, width, cols)
            s.wg[h] = part if k == 0 else s.wg[h] + part

    wg_core = remote(s.wg.at[1 - c], s.wg_c, s.wc.at[0], s.wc.at[1], other)
    wg_core.start()

    s.grad[plan.blocks] = jnp.zeros((width, BLK), BF16)
    for copy in grad_copies:
        copy.wait()
    back_copies = []
    for i, d in enumerate(plan.offsets):
        term = jnp.dot(s.grad[idx[plan.bh_r + i]], s.tiles[idx[plan.bh_t + i]], preferred_element_type=F32)
        s.bsend[i] = term.astype(BF16)
        copy = remote(
            s.bsend.at[i], s.brecv.at[i], s.back_s.at[i], s.back_r.at[i], (lax.rem(node + d + nn, nn), f)
        )
        copy.start()
        back_copies.append(copy)

    wg_core.wait()
    rows = width // xs
    for at in range(xs):
        s.wg1[at] = s.wg[c, :, pl.ds(at * rows, rows), :] + s.wg_c[:, pl.ds(at * rows, rows), :]
    x_copies = []
    for d in range(1, xs):
        to_x = lax.rem(x + d, xs)
        copy = remote(s.wg1.at[to_x], s.wg_x.at[d - 1], s.wx_s.at[d - 1], s.wx_r.at[d - 1], (node_of(z, to_x, c), f))
        copy.start()
        x_copies.append(copy)

    s.bsum[0] = jnp.zeros((width, BLK), F32)
    s.rsum[0] = jnp.zeros((width, BLK), F32)

    def backward_local(i, total):
        keep = idx[plan.bl_k + i].astype(F32)
        term = jnp.dot(s.grad[idx[plan.bl_r + i]], s.tiles[idx[plan.bl_t + i]], preferred_element_type=F32)
        total = total * keep + term
        s.bsum[i + 1] = total
        return total

    zero_t = jnp.zeros((width, BLK), F32)
    lax.fori_loop(0, plan.local, backward_local, zero_t, unroll=8)

    for copy in x_copies:
        copy.wait()
    mine = s.wg1[x]
    for d in range(1, xs):
        mine = mine + s.wg_x[d - 1]
    s.wg2[...] = mine
    z_copies = []
    for d in range(1, zs):
        to_z = lax.rem(z + d, zs)
        copy = remote(s.wg2.at[to_z], s.wg_z.at[d - 1], s.wz_s.at[d - 1], s.wz_r.at[d - 1], (node_of(to_z, x, c), f))
        copy.start()
        z_copies.append(copy)

    for copy in back_copies:
        copy.wait()

    def returned(i, total):
        keep = idx[plan.r_k + i].astype(F32)
        total = total * keep + s.brecv[idx[plan.r_s + i]].astype(F32)
        s.rsum[i + 1] = total
        return total

    lax.fori_loop(0, plan.halo, returned, zero_t, unroll=min(4, plan.halo))

    for copy in z_copies:
        copy.wait()
    mine = s.wg2[z]
    for d in range(1, zs):
        mine = mine + s.wg_z[d - 1]
    s.wg3[...] = mine
    away = lax.rem(z - f + nf, nf)

    @pl.when(away != 0)
    def _():
        remote(s.wg3, s.wg_y.at[away - 1], s.wy_s.at[0], s.wy_r.at[away - 1], (node, z)).start()

    def finish(b, _):
        out_ref[b] = (s.bsum[idx[plan.bl_end + b]] + s.rsum[idx[plan.r_end + b]]).astype(BF16)
        return 0

    lax.fori_loop(0, plan.blocks, finish, 0, unroll=4)

    z_from = f
    z_away = lax.rem(z - z_from + zs, zs)

    @pl.when(away != 0)
    def _():
        remote(s.wg3, s.wg_y.at[away - 1], s.wy_s.at[0], s.wy_r.at[away - 1], (node, z)).wait_send()
        remote(
            s.wg4, s.wg4, s.wb_s.at[z_away - 1], s.wb_r.at[z_away - 1], (node_of(z_from, x, c), f)
        ).wait_recv()

    @pl.when(away == 0)
    def _():
        total = s.wg3[...]
        for d in range(1, nf):
            remote(s.wg3, s.wg_y.at[d - 1], s.wy_s.at[0], s.wy_r.at[d - 1], (node, lax.rem(f + d, nf))).wait_recv()
            total = total + s.wg_y[d - 1]
        s.wg4[...] = total
        copies = []
        for d in range(1, zs):
            to = (node_of(lax.rem(z + d, zs), x, c), f)
            copies.append(remote(s.wg4, s.wg4, s.wb_s.at[d - 1], s.wb_r.at[d - 1], to))
        for copy in copies:
            copy.start()
        for copy in copies:
            copy.wait_send()

    s.wg5[c, x] = s.wg4[...]
    last_copies = []
    for i, (dx, dc) in enumerate(plane):
        to = (node_of(z, lax.rem(x + dx, xs), lax.rem(c + dc, CORES)), f)
        copy = remote(s.wg4, s.wg5.at[c, x], s.wl_s.at[i], s.wl_r.at[i], to)
        copy.start()
        last_copies.append(copy)
    for copy in last_copies:
        copy.wait()
    for h in range(CORES):
        for at in range(xs):
            wout_ref[pl.ds(at * rows, rows), pl.ds(h * cols, cols)] = s.wg5[h, at]


class Scratch:
    pass


def scratch_of(plan):
    nf, ns, halo, blocks, width = plan.feats, plan.stages, plan.halo, plan.blocks, plan.width
    cols, rows = plan.full // CORES, width // plan.xs
    dma = pltpu.SemaphoreType.DMA
    vmem = pltpu.VMEM
    return {
        "table": vmem((blocks + 1, BLK, width), BF16),
        "up": vmem((blocks, BLK, width), BF16),
        "upk": vmem((blocks // 2, BLK, 2 * width), BF16),
        "ur": vmem((ns, nf, BLK, 2 * width), BF16),
        "wh": vmem((CORES, nf, width // CORES, plan.full), BF16),
        "wfull": vmem((plan.full, plan.full), BF16),
        "tiles": vmem((plan.tiles, BLK, BLK), BF16),
        "hsend": vmem((halo, BLK // 2, 2 * width), BF16),
        "hrecv": vmem((halo, BLK // 2, 2 * width), BF16),
        "htable": vmem((halo, BLK, width), BF16),
        "fsum": vmem((plan.local + 1, BLK, width), F32),
        "hsum": vmem((halo + 1, BLK, width), F32),
        "apk": vmem((blocks // 2, BLK, 2 * width), BF16),
        "ar": vmem((ns, nf, BLK, 2 * width), BF16),
        "xrows": vmem((2 * BLK, plan.full), BF16),
        "gp": vmem((2 * BLK, plan.full), BF16),
        "gsend": vmem((ns, nf, 2, width, BLK), BF16),
        "grad": vmem((blocks + 1, width, BLK), BF16),
        "wg": vmem((CORES, nf, width, cols), F32),
        "wg_c": vmem((nf, width, cols), F32),
        "wg1": vmem((plan.xs, nf, rows, cols), F32),
        "wg_x": vmem((plan.xs - 1, nf, rows, cols), F32),
        "wg2": vmem((nf, rows, cols), F32),
        "wg_z": vmem((plan.zs - 1, rows, cols), F32),
        "wg3": vmem((rows, cols), F32),
        "wg_y": vmem((nf - 1, rows, cols), F32),
        "wg4": vmem((rows, cols), F32),
        "wg5": vmem((CORES, plan.xs, rows, cols), F32),
        "bsend": vmem((halo, width, BLK), BF16),
        "brecv": vmem((halo, width, BLK), BF16),
        "bsum": vmem((plan.local + 1, width, BLK), F32),
        "rsum": vmem((halo + 1, width, BLK), F32),
        "get": dma((4,)),
        "halo_s": dma((halo,)), "halo_r": dma((halo,)),
        "w_s": dma((nf - 1,)), "w_r": dma((nf - 1,)),
        "wx": dma((2,)),
        "up_s": dma((ns, nf - 1)), "up_r": dma((ns, nf - 1)),
        "ag_s": dma((ns, nf - 1)), "ag_r": dma((ns, nf - 1)),
        "gr_s": dma((ns, nf - 1)), "gr_r": dma((ns, nf - 1)),
        "back_s": dma((halo,)), "back_r": dma((halo,)),
        "wc": dma((2,)),
        "wx_s": dma((plan.xs - 1,)), "wx_r": dma((plan.xs - 1,)),
        "wz_s": dma((plan.zs - 1,)), "wz_r": dma((plan.zs - 1,)),
        "wy_s": dma((1,)), "wy_r": dma((nf - 1,)),
        "wb_s": dma((plan.zs - 1,)), "wb_r": dma((plan.zs - 1,)),
        "wl_s": dma((CORES * plan.xs - 1,)), "wl_r": dma((CORES * plan.xs - 1,)),
    }


def local(offsets_of, x_chips, features, weight, tile_row, tile_col, tile_count, send_blocks, tile_values, upstream):
    rows_dev, width = features.shape
    blocks = rows_dev // BLK
    nodes, feats = lax.axis_size("node"), lax.axis_size("feat")
    plan = Plan(blocks, width, tile_row.shape[0], feats, nodes, offsets_of(nodes), x_chips)
    idx = index_lists(plan, tile_row, tile_col, tile_count, send_blocks)
    scratch = scratch_of(plan)
    names = list(scratch)

    def body(idx, feats_hbm, up_hbm, w_hbm, tiles_hbm, out_ref, wout_ref, *refs):
        s = Scratch()
        for name, ref in zip(names, refs):
            setattr(s, name, ref)
        kernel(plan, idx, feats_hbm, up_hbm, w_hbm, tiles_hbm, out_ref, wout_ref, s)

    anywhere = pl.BlockSpec(memory_space=pl.ANY)
    in_vmem = pl.BlockSpec(memory_space=pltpu.VMEM)
    grad_t, weight_sum = pl.pallas_call(
        body,
        out_shape=(
            jax.ShapeDtypeStruct((blocks, width, BLK), BF16),
            jax.ShapeDtypeStruct((width, plan.full), F32),
        ),
        in_specs=[pl.BlockSpec(memory_space=pltpu.SMEM), anywhere, anywhere, anywhere, anywhere],
        out_specs=(in_vmem, in_vmem),
        scratch_shapes=[scratch[name] for name in names],
        compiler_params=pltpu.CompilerParams(
            collective_id=0, has_side_effects=True, vmem_limit_bytes=52 * 1024 * 1024
        ),
    )(idx, features.reshape(blocks, BLK, width), upstream.reshape(blocks, BLK, width), weight, tile_values)
    features_grad = jnp.swapaxes(grad_t, 1, 2).reshape(rows_dev, width)
    return features_grad, weight_sum / math.sqrt(rows_dev * nodes)


def build(mesh, offsets_of, x_chips):
    in_specs = (
        P("node", "feat"),
        P("feat", None),
        P("node"),
        P("node"),
        P("node"),
        P("node", None, None),
        P("node", None, None),
        P("node", "feat"),
    )
    out_specs = (P("node", "feat"), P("feat", None))
    return jax.shard_map(
        functools.partial(local, offsets_of, x_chips), mesh=mesh, in_specs=in_specs, out_specs=out_specs, check_vma=False
    )


def solution(mesh):
    return build(mesh, halo_offsets, X_CHIPS)
```

time: 473 us -> 99.7 us (0.21)
  waiting for transfers between devices: 305 us -> 0 us
  Pallas kernels: 0 us -> 86.3 us
  other arithmetic: 39.8 us -> 5.88 us
  local copies, waits for them, and re-layouts: 35.9 us -> 4.86 us
  starting transfers between devices: 26.2 us -> 0 us
  matrix products: 26 us -> 0 us
  blocking collectives: 23 us -> 0 us
  between operations: 14.6 us -> 1.4 us
    psum x1 -> x0, waiting for transfers between devices: 189 us -> none  [local(): weight_grad = lax.psum(grad_rows, 'node')]
    all_gather x2 -> x0, waiting for transfers between devices: 89.1 us -> none  [the longest x1 54.8 us: local(): shard_piece = lax.all_gather(grad_pre, 'feat', axis=1, tiled=True)]
    pallas_call x0 -> x1, Pallas kernels: none -> 86.3 us  [local(): pl.pallas_call(body, out_shape=(jax.ShapeDtypeStruct((blocks, width, BLK)...]
    all_to_all x2 -> x0, waiting for transfers between devices: 27.3 us -> none  [the longest x1 27.3 us: local(): lax.all_to_all(blocked[my_sends], 'node', split_axis=0, concat_axis=0, ti...]
    scatter-add x11 -> x0, other arithmetic: 27 us -> none  [the longest x5 13.4 us: backward_turn(): return scattered.at[col_ids].add(terms * alive[:, None, None])]
    all_to_all x2 -> x0, starting transfers between devices: 26 us -> none  [the longest x1 14.8 us: local(): lax.all_to_all(blocked[my_sends], 'node', split_axis=0, concat_axis=0, ti...]
    dot_general x13 -> x0, matrix products: 26 us -> none  [the longest x5 7.66 us: forward_turn(): jnp.einsum('tij,tjf->tif', tile_vals, sources, preferred_element_type=jnp...]
    gather x11 -> x0, local copies, waits for them, and re-layouts: 23.7 us -> none  [the longest x5 12.7 us: forward_turn(): sources = table[col_ids]]
  transfers between devices with their start and end apart: 5 -> 0, of which waited for: 4 -> 0; matrix products, arithmetic and copies ran while one was open for 2% -> 0% of each run, Pallas kernels for 0% -> 0%
where the time goes in v1:
time: 99.7 us; the launch traced here: 98.5 us
  Pallas kernels  86.3 us (87%)
  other arithmetic  5.88 us (6%)
  local copies, waits for them, and re-layouts  4.86 us (5%)
  between operations  1.4 us (1%)
    pallas_call x1, Pallas kernels, local(): pl.pallas_call(body, out_shape=(jax.ShapeDtypeStruct((blocks, width, BLK)...  86.3 us
    unnamed x4, local copies, waits for them, and re-layouts  3.9 us

profile of v1, /device:TPU:1, one launch (start us, length us, event | category | flops | bytes accessed | tf_op | source)
XLA Modules:
  0.0 98.5 jit_solution(9064037379720544255)
XLA Ops:
  0.6 0.0 copy-start
  1.3 0.7 and_select_fusion
  2.0 0.8 select_reduce_fusion.8
  2.9 0.2 convert_reduce_fusion.5
  3.1 0.1 select_reduce_fusion.6
  3.2 0.1 fusion.3
  3.3 0.1 compare_convert_fusion
  3.3 0.1 convert_reduce_fusion.4
  3.4 0.9 select_reduce_fusion.13
  4.3 0.2 convert_reduce_fusion.7
  4.5 0.2 select_reduce_fusion.9
  4.6 0.1 fusion.2
  4.7 0.1 compare_convert_fusion.2
  4.8 0.1 convert_reduce_fusion.6
  4.9 0.7 iota_add_fusion.3
  5.6 0.2 convert_reduce_fusion
  5.8 0.2 select_reduce_fusion
  6.0 0.1 fusion.1
  6.1 0.1 compare_convert_fusion.1
  6.2 0.1 convert_reduce_fusion.2
  6.3 0.1 fusion
  6.4 0.1 compare_convert_fusion.3
  6.5 0.1 convert_reduce_fusion.3
  6.6 0.1 concatenate.3.idx
  6.7 1.5 %copy.16 = bf16[4096,64]{1,0:T(8,128)(2,1)S(1)} copy(bf16[4096,64]{0,1:T(8,128)(2,1)} %param.9) | data formatting | bytes 1048576 | tf_op args[0]
  8.2 2.4 %copy.17 = bf16[4096,64]{1,0:T(8,128)(2,1)} copy(bf16[4096,64]{0,1:T(8,128)(2,1)} %param.16) | data formatting | bytes 1048576 | tf_op args[7]
  10.6 0.0 copy-done
  10.6 86.3 %shard_map.104 = (bf16[32,64,128]{2,1,0:T(8,128)(2,1)S(1)}, f32[64,512]{1,0:T(8,128)S(1)}) custom-call(s32[640]{0:T(1024)S(1)} %concatenate.3.idx, bf16[32,128,64]{2,1,0:T(8,128)(2,1)S(1)} %bitcast.12, bf16[32,128,64]{2,1,0:T(8,128)(2,1)} %bitcast.13, bf16[64,512]{1,0:T(8,128)(2,1)S(1)} %copy-done, bf16[80,128,128]{2,1,0:T(8,128)(2,1)} %tiles_hbm.1), custom_call_target="tpu_custom_call" | custom-call | tf_op jit(solution)/shard_map/pallas_call | solution.py:461
  96.9 0.9 copy_bitcast_fusion
  97.8 0.7 broadcast_multiply_fusion
  (7 shorter events, 0.0 us)
Async XLA Ops:
  0.6 10.0 %copy-start = (bf16[64,512]{1,0:T(8,128)(2,1)S(1)}, bf16[64,512]{1,0:T(8,128)(2,1)}, u32[]{:S(2)}) copy-start(bf16[64,512]{1,0:T(8,128)(2,1)} %w_hbm.1) | copy-start | bytes 196612

commit v2 on v1

v2 whole, which is shorter than its diff:
```python
import functools
import math

import jax
import jax.numpy as jnp
from jax import lax
from jax.experimental import pallas as pl
from jax.experimental.pallas import tpu as pltpu
from jax.sharding import PartitionSpec as P

MESH = pl.DeviceIdType.MESH
F32 = jnp.float32
BF16 = jnp.bfloat16
BLK = 128
CORES = 2
X_CHIPS = 4


def halo_offsets(node_count):
    near = [step for d in range(1, 8) for step in (d, -d)]
    return near + [8, 32]


class Plan:
    def __init__(self, blocks, width, tiles, feats, nodes, offsets, x_chips):
        self.blocks, self.width, self.tiles = blocks, width, tiles
        self.feats, self.nodes, self.offsets = feats, nodes, offsets
        self.halo = len(offsets)
        self.local = tiles - self.halo
        self.full = width * feats
        self.stages = blocks // (2 * feats)
        self.xs = x_chips
        self.zs = nodes // (CORES * x_chips)


LANES = 128
BITS = 7
MASK = (1 << BITS) - 1
(FL_T, FL_C, FL_K, FL_END, FH_T, FH_S, FH_K, FH_END, BH_T, BH_R, BL_T, BL_R, BL_K, BL_END, R_S, R_K, R_END) = range(17)
LISTS = 24


def iota(dim, rows=LANES):
    return lax.broadcasted_iota(jnp.int32, (rows, LANES), dim)


def as_columns(vector):
    return jnp.broadcast_to(vector, (LANES, LANES)).T


def count(where):
    return jnp.sum(jnp.where(where, 1, 0), axis=0, keepdims=True)


def pick(one_hot, columns):
    return jnp.sum(jnp.where(one_hot, columns, 0), axis=0, keepdims=True)


def in_order(group, first, second):
    lane, sub = iota(1), iota(0)
    down = as_columns(group)
    smaller = count(down < group)
    rank = smaller + count(jnp.logical_and(down == group, sub < lane))
    follows = jnp.where(rank > smaller, 1, 0)
    packed = as_columns(rank + (first << BITS) + (second << (2 * BITS)) + (follows << (3 * BITS)))
    got = pick((packed & MASK) == lane, packed >> BITS)
    end = jnp.where(count(down == lane) > 0, count(down <= lane), 0)
    return got & MASK, (got >> BITS) & MASK, got >> (2 * BITS), end


def write_lists(plan, node, live, row_ref, col_ref, send_ref, line, lists):
    n = plan.nodes
    lane = iota(1, 1)
    line[...] = jnp.zeros_like(line)
    line[0:1, 0 : plan.tiles] = row_ref[...]
    line[1:2, 0 : plan.tiles] = col_ref[...]
    line[2:3, 0:n] = send_ref[...]
    row, col, sends = line[0:1, :], line[1:2, :], line[2:3, :]
    alive = lane < live
    local = jnp.logical_and(alive, col < plan.blocks)
    row_in, col_in = jnp.where(local, row, plan.blocks), jnp.where(local, col, plan.blocks)
    fl_t, fl_c, fl_k, fl_end = in_order(row_in, lane, col_in)
    bl_t, bl_r, bl_k, bl_end = in_order(col_in, lane, row_in)

    reads, serves = jnp.full((1, LANES), -1, jnp.int32), jnp.full((1, LANES), -1, jnp.int32)
    for i, d in enumerate(plan.offsets):
        reads = jnp.where(lane == i, plan.blocks + lax.rem(node + d + n, n), reads)
        serves = jnp.where(lane == i, lax.rem(node - d + n, n), serves)
    packed = as_columns(jnp.where(alive, col + (row << BITS), 0))
    got = pick((packed & MASK) == reads, (packed >> BITS) + (iota(0) << BITS))
    bh_t, bh_r = got >> BITS, got & MASK
    target = pick(iota(0) == serves, as_columns(sends))
    used = lane < plan.halo
    fh_t, fh_s, fh_k, fh_end = in_order(jnp.where(used, bh_r, plan.blocks), bh_t, lane)
    r_s, _, r_k, r_end = in_order(jnp.where(used, target, plan.blocks), lane, lane)
    rows = [fl_t, fl_c, fl_k, fl_end, fh_t, fh_s, fh_k, fh_end, bh_t, bh_r, bl_t, bl_r, bl_k, bl_end, r_s, r_k, r_end]
    lists[...] = jnp.zeros_like(lists)
    for i, vector in enumerate(rows):
        lists[i : i + 1, :] = vector


def kernel(plan, count_ref, send_sm, row_ref, col_ref, send_ref, feats_hbm, up_hbm, w_hbm, tiles_hbm, out_ref, wout_ref, s):
    nf, nn, width = plan.feats, plan.nodes, plan.width
    zs, xs = plan.zs, plan.xs
    rows, cols = width // xs, plan.full // CORES
    pair = 2 * BLK
    node, f = lax.axis_index("node"), lax.axis_index("feat")
    c = lax.rem(node, CORES)
    x = lax.rem(node // CORES, xs)
    z = node // (CORES * xs)
    idx = s.idx

    def node_of(z_at, x_at, c_at):
        return (z_at * xs + x_at) * CORES + c_at

    def remote(src, dst, send_sem, recv_sem, to):
        return pltpu.make_async_remote_copy(
            src_ref=src, dst_ref=dst, send_sem=send_sem, recv_sem=recv_sem, device_id=to, device_id_type=MESH
        )

    def up_pair(p):
        return up_hbm.at[:, pl.ds(pl.multiple_of(p * pair, pair), pair)]

    get_feats = pltpu.make_async_copy(feats_hbm, s.feats, s.get.at[0])
    get_w = pltpu.make_async_copy(
        w_hbm.at[pl.ds(x * rows, rows), pl.ds(pl.multiple_of(c * cols, cols), cols)], s.wq.at[c, x, f], s.get.at[1]
    )
    get_tiles = pltpu.make_async_copy(tiles_hbm, s.tiles, s.get.at[2])
    get_up = [pltpu.make_async_copy(up_pair(k * nf + f), s.ur.at[k, f], s.get.at[3 + k]) for k in range(plan.stages)]
    for copy in [get_feats, get_w, get_tiles] + get_up:
        copy.start()

    near = sorted({d % nn for d in plan.offsets} | {-d % nn for d in plan.offsets})
    plane = [(dx, dc) for dx in range(xs) for dc in range(CORES) if dx or dc]
    partners = [(node_of(lax.rem(z + d, zs), x, c), f) for d in range(1, zs)]
    partners += [(lax.rem(node + d, nn), f) for d in near]
    partners += [(node_of(z, lax.rem(x + dx, xs), lax.rem(c + dc, CORES)), f) for dx, dc in plane]
    partners += [(node, lax.rem(f + d, nf)) for d in range(1, nf)]
    barrier = pltpu.get_barrier_semaphore()
    for to in partners:
        pl.semaphore_signal(barrier, inc=1, device_id=to, device_id_type=MESH)

    get_w.wait()
    pl.semaphore_wait(barrier, len(partners))

    far_first = sorted(range(1, nf), key=lambda d: -min(d, nf - d))
    w_copies = [
        remote(s.wq.at[c, x, f], s.wq.at[c, x, f], s.w_s.at[d - 1], s.w_r.at[d - 1], (node, lax.rem(f + d, nf)))
        for d in far_first
    ]
    up_copies = []
    for k in range(plan.stages):
        stage_copies = []
        for d in far_first:
            j = lax.rem(f + d, nf)
            stage_copies.append(
                remote(up_pair(k * nf + j), s.ur.at[k, f], s.up_s.at[k, d - 1], s.up_r.at[k, d - 1], (node, j))
            )
        up_copies.append(stage_copies)
    for copy in w_copies + up_copies[0]:
        copy.start()
    get_feats.wait()
    for b in range(plan.blocks):
        s.table[b] = s.feats[:, b * BLK : (b + 1) * BLK]
    s.table[plan.blocks] = jnp.zeros((width, BLK), BF16)
    halo_copies = []
    for i, d in enumerate(plan.offsets):
        to = lax.rem(node - d + nn, nn)
        s.hsend[i] = s.table[send_sm[0, to]]
        copy = remote(s.hsend.at[i], s.hrecv.at[i], s.halo_s.at[i], s.halo_r.at[i], (to, f))
        copy.start()
        halo_copies.append(copy)
    for copy in sum(up_copies[1:], []):
        copy.start()

    write_lists(plan, node, count_ref[0], row_ref, col_ref, send_ref, s.line, s.lists)
    put_lists = pltpu.make_async_copy(s.lists, s.idx, s.get.at[3 + plan.stages])
    put_lists.start()
    zero = jnp.zeros((width, BLK), F32)
    for ref in (s.fsum, s.hsum, s.bsum, s.rsum):
        ref[0] = zero
    s.grad[plan.blocks] = jnp.zeros((width, BLK), BF16)

    for copy in w_copies:
        copy.wait()
    wx_copies = []
    for d in range(1, xs):
        to = (node_of(z, lax.rem(x + d, xs), c), f)
        wx_copies.append(remote(s.wq.at[c, x], s.wq.at[c, x], s.wqx_s.at[d - 1], s.wqx_r.at[d - 1], to))
    for copy in wx_copies:
        copy.start()

    put_lists.wait()
    get_tiles.wait()

    def forward_local(i, total):
        keep = idx[FL_K, i].astype(F32)
        term = lax.dot_general(
            s.table[idx[FL_C, i]], s.tiles[idx[FL_T, i]], (((1,), (1,)), ((), ())), preferred_element_type=F32
        )
        total = total * keep + term
        s.fsum[i + 1] = total
        return total

    lax.fori_loop(0, plan.local, forward_local, zero, unroll=16)

    for copy in halo_copies:
        copy.wait()

    def forward_halo(i, total):
        keep = idx[FH_K, i].astype(F32)
        term = lax.dot_general(
            s.hrecv[idx[FH_S, i]], s.tiles[idx[FH_T, i]], (((1,), (1,)), ((), ())), preferred_element_type=F32
        )
        total = total * keep + term
        s.hsum[i + 1] = total
        return total

    lax.fori_loop(0, plan.halo, forward_halo, zero, unroll=plan.halo)

    def summed(b):
        return (s.fsum[idx[FL_END, b]] + s.hsum[idx[FH_END, b]]).astype(BF16)

    agg_copies = []
    for k in range(plan.stages):
        stage_copies = []
        for d in far_first + [0]:
            j = lax.rem(f + d, nf)
            p = k * nf + j
            into = s.apk.at[p] if d else s.ar.at[k, f]
            into[:, 0:BLK] = summed(2 * p)
            into[:, BLK:pair] = summed(2 * p + 1)
            if d:
                copy = remote(s.apk.at[p], s.ar.at[k, f], s.ag_s.at[k, d - 1], s.ag_r.at[k, d - 1], (node, j))
                copy.start()
                stage_copies.append(copy)
        agg_copies.append(stage_copies)

    for copy in wx_copies:
        copy.wait()
    other = (node_of(z, x, 1 - c), f)
    w_swap = remote(s.wq.at[c], s.wq.at[c], s.wsw.at[0], s.wsw.at[1], other)
    w_swap.start()
    w_swap.wait()
    for j in range(nf):
        for at in range(xs):
            for h in range(CORES):
                s.wfull[pl.ds(j * width + at * rows, rows), pl.ds(h * cols, cols)] = s.wq[h, at, j]
    s.wt[...] = s.wfull[...].T

    grad_copies = []
    for k in range(plan.stages):
        get_up[k].wait()
        for copy in up_copies[k] + agg_copies[k]:
            copy.wait()
        agg = s.ar[k].reshape(plan.full, pair)
        pre = jnp.dot(s.wt[...], agg, preferred_element_type=F32)
        sig = jax.nn.sigmoid(pre)
        upstream = s.ur[k].reshape(plan.full, pair).astype(F32)
        s.gp[...] = (upstream * sig * (1.0 + pre * (1.0 - sig))).astype(BF16)

        def weight_part():
            wg = lax.dot_general(agg, s.gp[...], (((1,), (1,)), ((), ())), preferred_element_type=F32)
            for h in range(CORES):
                part = wg[:, h * cols : (h + 1) * cols].reshape(nf, width, cols)
                s.wg[h] = part if k == 0 else s.wg[h] + part

        last = k == plan.stages - 1
        if last:
            weight_part()
            wg_core = remote(s.wg.at[1 - c], s.wg_c, s.wc.at[0], s.wc.at[1], other)
            wg_core.start()
        grad = jnp.dot(s.wfull[...], s.gp[...], preferred_element_type=F32).astype(BF16)
        for j in range(nf):
            for h in range(2):
                s.gsend[k, j, h] = grad[j * width : (j + 1) * width, h * BLK : (h + 1) * BLK]
        for d in far_first:
            j = lax.rem(f + d, nf)
            copy = remote(
                s.gsend.at[k, j], s.grad.at[pl.ds(2 * (k * nf + f), 2)], s.gr_s.at[k, d - 1], s.gr_r.at[k, d - 1], (node, j)
            )
            copy.start()
            grad_copies.append(copy)
        s.grad[pl.ds(2 * (k * nf + f), 2)] = s.gsend[k, f]
        if not last:
            weight_part()

    wg_core.wait()
    x_copies = []
    for d in list(range(1, xs)) + [0]:
        to_x = lax.rem(x + d, xs)
        at = pl.ds(pl.multiple_of(to_x * rows, rows), rows)
        part = s.wg[c, :, at, :] + s.wg_c[:, at, :]
        if d:
            s.wg1[d - 1] = part.astype(BF16)
            to = (node_of(z, to_x, c), f)
            copy = remote(s.wg1.at[d - 1], s.wg_x.at[d - 1], s.wx_s.at[d - 1], s.wx_r.at[d - 1], to)
            copy.start()
            x_copies.append(copy)
        else:
            s.wg2[...] = part
    for copy in x_copies:
        copy.wait()
    s.wg2[...] = sum([s.wg_x[d].astype(F32) for d in range(xs - 1)], s.wg2[...])
    z_copies = []
    for d in range(1, zs):
        to_z = lax.rem(z + d, zs)
        copy = remote(s.wg2.at[to_z], s.wg_z.at[d - 1], s.wz_s.at[d - 1], s.wz_r.at[d - 1], (node_of(to_z, x, c), f))
        copy.start()
        z_copies.append(copy)

    for copy in grad_copies:
        copy.wait()
    back_copies = []
    for i, d in enumerate(plan.offsets):
        term = jnp.dot(s.grad[idx[BH_R, i]], s.tiles[idx[BH_T, i]], preferred_element_type=F32)
        s.bsend[i] = term.astype(BF16)
        copy = remote(
            s.bsend.at[i], s.brecv.at[i], s.back_s.at[i], s.back_r.at[i], (lax.rem(node + d + nn, nn), f)
        )
        copy.start()
        back_copies.append(copy)

    for copy in z_copies:
        copy.wait()
    s.wg3[...] = sum([s.wg_z[d] for d in range(zs - 1)], s.wg2[z])
    away = lax.rem(z - f + nf, nf)

    @pl.when(away != 0)
    def _():
        remote(s.wg3, s.wg_y.at[away - 1], s.wy_s.at[0], s.wy_r.at[away - 1], (node, z)).start()

    def backward_local(i, total):
        keep = idx[BL_K, i].astype(F32)
        term = jnp.dot(s.grad[idx[BL_R, i]], s.tiles[idx[BL_T, i]], preferred_element_type=F32)
        total = total * keep + term
        s.bsum[i + 1] = total
        return total

    lax.fori_loop(0, plan.local, backward_local, zero, unroll=16)

    @pl.when(away != 0)
    def _():
        remote(s.wg3, s.wg_y.at[away - 1], s.wy_s.at[0], s.wy_r.at[away - 1], (node, z)).wait_send()

    @pl.when(away == 0)
    def _():
        total = s.wg3[...]
        for d in range(1, nf):
            remote(s.wg3, s.wg_y.at[d - 1], s.wy_s.at[0], s.wy_r.at[d - 1], (node, lax.rem(f + d, nf))).wait_recv()
            total = total + s.wg_y[d - 1]
        s.wg4[...] = total
        for d in range(1, zs):
            to = (node_of(lax.rem(z + d, zs), x, c), f)
            remote(s.wg4, s.wg4, s.wb_s.at[d - 1], s.wb_r.at[d - 1], to).start()

    for copy in back_copies:
        copy.wait()

    def returned(i, total):
        keep = idx[R_K, i].astype(F32)
        total = total * keep + s.brecv[idx[R_S, i]].astype(F32)
        s.rsum[i + 1] = total
        return total

    lax.fori_loop(0, plan.halo, returned, zero, unroll=plan.halo)

    @pl.when(away != 0)
    def _():
        remote(s.wg4, s.wg4, s.wb_s.at[away - 1], s.wb_r.at[away - 1], (node_of(f, x, c), f)).wait_recv()

    @pl.when(away == 0)
    def _():
        for d in range(1, zs):
            to = (node_of(lax.rem(z + d, zs), x, c), f)
            remote(s.wg4, s.wg4, s.wb_s.at[d - 1], s.wb_r.at[d - 1], to).wait_send()

    s.wg5[c, x] = s.wg4[...]
    last_copies = []
    for i, (dx, dc) in enumerate(plane):
        to = (node_of(z, lax.rem(x + dx, xs), lax.rem(c + dc, CORES)), f)
        copy = remote(s.wg4, s.wg5.at[c, x], s.wl_s.at[i], s.wl_r.at[i], to)
        copy.start()
        last_copies.append(copy)
    for b in range(plan.blocks):
        out_ref[:, b * BLK : (b + 1) * BLK] = (s.bsum[idx[BL_END, b]] + s.rsum[idx[R_END, b]]).astype(BF16)

    for copy in last_copies:
        copy.wait()
    for h in range(CORES):
        for at in range(xs):
            wout_ref[pl.ds(at * rows, rows), pl.ds(h * cols, cols)] = s.wg5[h, at]


class Scratch:
    pass


def scratch_of(plan):
    nf, ns, halo, blocks, width = plan.feats, plan.stages, plan.halo, plan.blocks, plan.width
    cols, rows = plan.full // CORES, width // plan.xs
    dma = pltpu.SemaphoreType.DMA
    vmem = pltpu.VMEM
    return {
        "feats": vmem((width, blocks * BLK), BF16),
        "table": vmem((blocks + 1, width, BLK), BF16),
        "ur": vmem((ns, nf, width, 2 * BLK), BF16),
        "wq": vmem((CORES, plan.xs, nf, rows, cols), BF16),
        "wfull": vmem((plan.full, plan.full), BF16),
        "wt": vmem((plan.full, plan.full), BF16),
        "tiles": vmem((plan.tiles, BLK, BLK), BF16),
        "hsend": vmem((halo, width, BLK), BF16),
        "hrecv": vmem((halo, width, BLK), BF16),
        "fsum": vmem((plan.local + 1, width, BLK), F32),
        "hsum": vmem((halo + 1, width, BLK), F32),
        "apk": vmem((blocks // 2, width, 2 * BLK), BF16),
        "ar": vmem((ns, nf, width, 2 * BLK), BF16),
        "gp": vmem((plan.full, 2 * BLK), BF16),
        "gsend": vmem((ns, nf, 2, width, BLK), BF16),
        "grad": vmem((blocks + 1, width, BLK), BF16),
        "line": vmem((8, LANES), jnp.int32),
        "lists": vmem((LISTS, LANES), jnp.int32),
        "idx": pltpu.SMEM((LISTS, LANES), jnp.int32),
        "wg": vmem((CORES, nf, width, cols), F32),
        "wg_c": vmem((nf, width, cols), F32),
        "wg1": vmem((plan.xs - 1, nf, rows, cols), BF16),
        "wg_x": vmem((plan.xs - 1, nf, rows, cols), BF16),
        "wg2": vmem((nf, rows, cols), F32),
        "wg_z": vmem((plan.zs - 1, rows, cols), F32),
        "wg3": vmem((rows, cols), F32),
        "wg_y": vmem((nf - 1, rows, cols), F32),
        "wg4": vmem((rows, cols), F32),
        "wg5": vmem((CORES, plan.xs, rows, cols), F32),
        "bsend": vmem((halo, width, BLK), BF16),
        "brecv": vmem((halo, width, BLK), BF16),
        "bsum": vmem((plan.local + 1, width, BLK), F32),
        "rsum": vmem((halo + 1, width, BLK), F32),
        "get": dma((4 + ns,)),
        "halo_s": dma((halo,)), "halo_r": dma((halo,)),
        "w_s": dma((nf - 1,)), "w_r": dma((nf - 1,)),
        "wqx_s": dma((plan.xs - 1,)), "wqx_r": dma((plan.xs - 1,)),
        "wsw": dma((2,)),
        "up_s": dma((ns, nf - 1)), "up_r": dma((ns, nf - 1)),
        "ag_s": dma((ns, nf - 1)), "ag_r": dma((ns, nf - 1)),
        "gr_s": dma((ns, nf - 1)), "gr_r": dma((ns, nf - 1)),
        "back_s": dma((halo,)), "back_r": dma((halo,)),
        "wc": dma((2,)),
        "wx_s": dma((plan.xs - 1,)), "wx_r": dma((plan.xs - 1,)),
        "wz_s": dma((plan.zs - 1,)), "wz_r": dma((plan.zs - 1,)),
        "wy_s": dma((1,)), "wy_r": dma((nf - 1,)),
        "wb_s": dma((plan.zs - 1,)), "wb_r": dma((plan.zs - 1,)),
        "wl_s": dma((CORES * plan.xs - 1,)), "wl_r": dma((CORES * plan.xs - 1,)),
    }


def local(offsets_of, x_chips, features, weight, tile_row, tile_col, tile_count, send_blocks, tile_values, upstream):
    rows_dev, width = features.shape
    blocks = rows_dev // BLK
    nodes, feats = lax.axis_size("node"), lax.axis_size("feat")
    plan = Plan(blocks, width, tile_row.shape[0], feats, nodes, offsets_of(nodes), x_chips)
    scratch = scratch_of(plan)
    names = list(scratch)
    given = 9

    def body(*refs):
        s = Scratch()
        for name, ref in zip(names, refs[given + 2 :]):
            setattr(s, name, ref)
        kernel(plan, *refs[: given + 2], s)

    anywhere = pl.BlockSpec(memory_space=pltpu.HBM)
    in_vmem = pl.BlockSpec(memory_space=pltpu.VMEM)
    in_smem = pl.BlockSpec(memory_space=pltpu.SMEM)
    sends = send_blocks.reshape(1, nodes)
    grad_t, weight_sum = pl.pallas_call(
        body,
        out_shape=(
            pltpu.VMEM((width, rows_dev), BF16),
            pltpu.VMEM((width, plan.full), F32),
        ),
        in_specs=[in_smem, in_smem, in_vmem, in_vmem, in_vmem, anywhere, anywhere, anywhere, anywhere],
        out_specs=(in_vmem, in_vmem),
        scratch_shapes=[scratch[name] for name in names],
        compiler_params=pltpu.CompilerParams(
            collective_id=0, has_side_effects=True, vmem_limit_bytes=62 * 1024 * 1024
        ),
    )(
        tile_count, sends, tile_row.reshape(1, -1), tile_col.reshape(1, -1), sends,
        features.T, upstream.T, weight, tile_values,
    )
    return grad_t.T, weight_sum / math.sqrt(rows_dev * nodes)


def build(mesh, offsets_of, x_chips):
    in_specs = (
        P("node", "feat"),
        P("feat", None),
        P("node"),
        P("node"),
        P("node"),
        P("node", None, None),
        P("node", None, None),
        P("node", "feat"),
    )
    out_specs = (P("node", "feat"), P("feat", None))
    return jax.shard_map(
        functools.partial(local, offsets_of, x_chips), mesh=mesh, in_specs=in_specs, out_specs=out_specs, check_vma=False
    )


def solution(mesh):
    return build(mesh, halo_offsets, X_CHIPS)
```

time: 99.7 us -> 73.9 us (0.74)
  the two profiles are of different devices: /device:TPU:1 before, /device:TPU:33 now
where the time goes in v2:
time: 73.9 us; the launch traced here: 73.7 us
  Pallas kernels  71 us (96%)
  between operations  1.29 us (2%)
  local copies, waits for them, and re-layouts  0.8 us (1%)
    pallas_call x1, Pallas kernels, local(): pl.pallas_call(body, out_shape=(pltpu.VMEM((width, rows_dev), BF16), pltp...  71 us

profile of v2, /device:TPU:33, one launch (start us, length us, event | category | flops | bytes accessed | tf_op | source)
XLA Modules:
  0.0 73.7 jit_solution(12339772904846672698)
XLA Ops:
  1.3 71.0 %shard_map.95 = (bf16[64,4096]{1,0:T(8,128)(2,1)S(1)}, f32[64,512]{1,0:T(8,128)S(1)}) custom-call(s32[1]{0:T(128)S(6)} %copy.12.refs_0_, s32[1,64]{1,0:T(1,128)} %bitcast.9, s32[1,80]{1,0:T(1,128)} %bitcast.11, s32[1,80]{1,0:T(1,128)} %bitcast.12, s32[1,64]{1,0:T(1,128)} %bitcast.10, bf16[64,4096]{1,0:T(8,128)(2,1)} %bitcast.7, bf16[64,4096]{1,0:T(8,128)(2,1)} %bitcast.8, ...), custom_call_target="tpu_custom_call" | custom-call | tf_op jit(solution)/shard_map/pallas_call | solution.py:475
  72.3 0.8 %copy.11 = bf16[4096,64]{0,1:T(8,128)(2,1)} copy(bf16[4096,64]{0,1:T(8,128)(2,1)S(1)} %bitcast.6) | data formatting | bytes 1048576
  73.1 0.7 broadcast_multiply_fusion

commit v3 on v2

--- a/solution.py
+++ b/solution.py
@@ -99,7 +99,7 @@
         lists[i : i + 1, :] = vector
 
 
-def kernel(plan, count_ref, send_sm, row_ref, col_ref, send_ref, feats_hbm, up_hbm, w_hbm, tiles_hbm, out_ref, wout_ref, s):
+def kernel(plan, count_hbm, send_hbm, row_hbm, col_hbm, feats_hbm, up_hbm, w_hbm, tiles_hbm, out_ref, wout_ref, s):
     nf, nn, width = plan.feats, plan.nodes, plan.width
     zs, xs = plan.zs, plan.xs
     rows, cols = width // xs, plan.full // CORES
@@ -127,7 +127,14 @@
     )
     get_tiles = pltpu.make_async_copy(tiles_hbm, s.tiles, s.get.at[2])
     get_up = [pltpu.make_async_copy(up_pair(k * nf + f), s.ur.at[k, f], s.get.at[3 + k]) for k in range(plan.stages)]
-    for copy in [get_feats, get_w, get_tiles] + get_up:
+    get_send = pltpu.make_async_copy(send_hbm, s.send_sm, s.get_small.at[0])
+    get_lines = [
+        pltpu.make_async_copy(src, dst, s.get_small.at[1 + i])
+        for i, (src, dst) in enumerate(
+            [(send_hbm, s.send_v), (row_hbm, s.row_v), (col_hbm, s.col_v), (count_hbm, s.count_v)]
+        )
+    ]
+    for copy in [get_w, get_send, get_feats, get_tiles] + get_up + get_lines:
         copy.start()
 
     near = sorted({d % nn for d in plan.offsets} | {-d % nn for d in plan.offsets})
@@ -160,20 +167,23 @@
     for copy in w_copies + up_copies[0]:
         copy.start()
     get_feats.wait()
+    get_send.wait()
     for b in range(plan.blocks):
         s.table[b] = s.feats[:, b * BLK : (b + 1) * BLK]
     s.table[plan.blocks] = jnp.zeros((width, BLK), BF16)
     halo_copies = []
     for i, d in enumerate(plan.offsets):
         to = lax.rem(node - d + nn, nn)
-        s.hsend[i] = s.table[send_sm[0, to]]
+        s.hsend[i] = s.table[s.send_sm[0, to]]
         copy = remote(s.hsend.at[i], s.hrecv.at[i], s.halo_s.at[i], s.halo_r.at[i], (to, f))
         copy.start()
         halo_copies.append(copy)
     for copy in sum(up_copies[1:], []):
         copy.start()
 
-    write_lists(plan, node, count_ref[0], row_ref, col_ref, send_ref, s.line, s.lists)
+    for copy in get_lines:
+        copy.wait()
+    write_lists(plan, node, s.count_v[...], s.row_v, s.col_v, s.send_v, s.line, s.lists)
     put_lists = pltpu.make_async_copy(s.lists, s.idx, s.get.at[3 + plan.stages])
     put_lists.start()
     zero = jnp.zeros((width, BLK), F32)
@@ -249,31 +259,8 @@
     s.wt[...] = s.wfull[...].T
 
     grad_copies = []
-    for k in range(plan.stages):
-        get_up[k].wait()
-        for copy in up_copies[k] + agg_copies[k]:
-            copy.wait()
-        agg = s.ar[k].reshape(plan.full, pair)
-        pre = jnp.dot(s.wt[...], agg, preferred_element_type=F32)
-        sig = jax.nn.sigmoid(pre)
-        upstream = s.ur[k].reshape(plan.full, pair).astype(F32)
-        s.gp[...] = (upstream * sig * (1.0 + pre * (1.0 - sig))).astype(BF16)
-
-        def weight_part():
-            wg = lax.dot_general(agg, s.gp[...], (((1,), (1,)), ((), ())), preferred_element_type=F32)
-            for h in range(CORES):
-                part = wg[:, h * cols : (h + 1) * cols].reshape(nf, width, cols)
-                s.wg[h] = part if k == 0 else s.wg[h] + part
-
-        last = k == plan.stages - 1
-        if last:
-            weight_part()
-            wg_core = remote(s.wg.at[1 - c], s.wg_c, s.wc.at[0], s.wc.at[1], other)
-            wg_core.start()
-        grad = jnp.dot(s.wfull[...], s.gp[...], preferred_element_type=F32).astype(BF16)
-        for j in range(nf):
-            for h in range(2):
-                s.gsend[k, j, h] = grad[j * width : (j + 1) * width, h * BLK : (h + 1) * BLK]
+
+    def send_grad(k):
         for d in far_first:
             j = lax.rem(f + d, nf)
             copy = remote(
@@ -281,6 +268,37 @@
             )
             copy.start()
             grad_copies.append(copy)
+
+    for k in range(plan.stages):
+        get_up[k].wait()
+        for copy in up_copies[k] + agg_copies[k]:
+            copy.wait()
+        if k:
+            send_grad(k - 1)
+        agg = s.ar[k].reshape(plan.full, pair)
+        pre = jnp.dot(s.wt[...], agg, preferred_element_type=F32)
+        sig = jax.nn.sigmoid(pre)
+        upstream = s.ur[k].reshape(plan.full, pair).astype(F32)
+        s.gp[...] = (upstream * sig * (1.0 + pre * (1.0 - sig))).astype(BF16)
+
+        def weight_part():
+            wg = lax.dot_general(agg, s.gp[...], (((1,), (1,)), ((), ())), preferred_element_type=F32)
+            for h in range(CORES):
+                part = wg[:, h * cols : (h + 1) * cols].reshape(nf, width, cols)
+                s.wg[h] = part if k == 0 else s.wg[h] + part
+
+        last = k == plan.stages - 1
+        if last:
+            weight_part()
+            s.wg0[...] = s.wg[1 - c].astype(BF16)
+            wg_core = remote(s.wg0, s.wg_c, s.wc.at[0], s.wc.at[1], other)
+            wg_core.start()
+        grad = jnp.dot(s.wfull[...], s.gp[...], preferred_element_type=F32).astype(BF16)
+        for j in range(nf):
+            for h in range(2):
+                s.gsend[k, j, h] = grad[j * width : (j + 1) * width, h * BLK : (h + 1) * BLK]
+        if last:
+            send_grad(k)
         s.grad[pl.ds(2 * (k * nf + f), 2)] = s.gsend[k, f]
         if not last:
             weight_part()
@@ -290,7 +308,7 @@
     for d in list(range(1, xs)) + [0]:
         to_x = lax.rem(x + d, xs)
         at = pl.ds(pl.multiple_of(to_x * rows, rows), rows)
-        part = s.wg[c, :, at, :] + s.wg_c[:, at, :]
+        part = s.wg[c, :, at, :] + s.wg_c[:, at, :].astype(F32)
         if d:
             s.wg1[d - 1] = part.astype(BF16)
             to = (node_of(z, to_x, c), f)
@@ -302,10 +320,21 @@
     for copy in x_copies:
         copy.wait()
     s.wg2[...] = sum([s.wg_x[d].astype(F32) for d in range(xs - 1)], s.wg2[...])
+    s.wg2b[...] = s.wg2[...].astype(BF16)
+    y_copies = []
+    for d in far_first:
+        j = lax.rem(f + d, nf)
+        copy = remote(s.wg2b.at[j], s.wg_y.at[d - 1], s.wy_s.at[d - 1], s.wy_r.at[d - 1], (node, j))
+        copy.start()
+        y_copies.append(copy)
+    for copy in y_copies:
+        copy.wait()
+    s.wg3[...] = sum([s.wg_y[d].astype(F32) for d in range(nf - 1)], s.wg2[f]).astype(BF16)
+    s.wg_z[z] = s.wg3[...]
     z_copies = []
     for d in range(1, zs):
-        to_z = lax.rem(z + d, zs)
-        copy = remote(s.wg2.at[to_z], s.wg_z.at[d - 1], s.wz_s.at[d - 1], s.wz_r.at[d - 1], (node_of(to_z, x, c), f))
+        to = (node_of(lax.rem(z + d, zs), x, c), f)
+        copy = remote(s.wg3, s.wg_z.at[z], s.wz_s.at[d - 1], s.wz_r.at[d - 1], to)
         copy.start()
         z_copies.append(copy)
 
@@ -321,15 +350,6 @@
         copy.start()
         back_copies.append(copy)
 
-    for copy in z_copies:
-        copy.wait()
-    s.wg3[...] = sum([s.wg_z[d] for d in range(zs - 1)], s.wg2[z])
-    away = lax.rem(z - f + nf, nf)
-
-    @pl.when(away != 0)
-    def _():
-        remote(s.wg3, s.wg_y.at[away - 1], s.wy_s.at[0], s.wy_r.at[away - 1], (node, z)).start()
-
     def backward_local(i, total):
         keep = idx[BL_K, i].astype(F32)
         term = jnp.dot(s.grad[idx[BL_R, i]], s.tiles[idx[BL_T, i]], preferred_element_type=F32)
@@ -337,22 +357,21 @@
         s.bsum[i + 1] = total
         return total
 
-    lax.fori_loop(0, plan.local, backward_local, zero, unroll=16)
-
-    @pl.when(away != 0)
-    def _():
-        remote(s.wg3, s.wg_y.at[away - 1], s.wy_s.at[0], s.wy_r.at[away - 1], (node, z)).wait_send()
-
-    @pl.when(away == 0)
-    def _():
-        total = s.wg3[...]
-        for d in range(1, nf):
-            remote(s.wg3, s.wg_y.at[d - 1], s.wy_s.at[0], s.wy_r.at[d - 1], (node, lax.rem(f + d, nf))).wait_recv()
-            total = total + s.wg_y[d - 1]
-        s.wg4[...] = total
-        for d in range(1, zs):
-            to = (node_of(lax.rem(z + d, zs), x, c), f)
-            remote(s.wg4, s.wg4, s.wb_s.at[d - 1], s.wb_r.at[d - 1], to).start()
+    middle = plan.local // 2
+    total = lax.fori_loop(0, middle, backward_local, zero, unroll=16)
+
+    for copy in z_copies:
+        copy.wait()
+    s.wg4[...] = sum([s.wg_z[at].astype(F32) for at in range(1, zs)], s.wg_z[0].astype(F32))
+    s.wg5[c, x] = s.wg4[...]
+    last_copies = []
+    for i, (dx, dc) in enumerate(plane):
+        to = (node_of(z, lax.rem(x + dx, xs), lax.rem(c + dc, CORES)), f)
+        copy = remote(s.wg4, s.wg5.at[c, x], s.wl_s.at[i], s.wl_r.at[i], to)
+        copy.start()
+        last_copies.append(copy)
+
+    lax.fori_loop(middle, plan.local, backward_local, total, unroll=16)
 
     for copy in back_copies:
         copy.wait()
@@ -365,23 +384,6 @@
 
     lax.fori_loop(0, plan.halo, returned, zero, unroll=plan.halo)
 
-    @pl.when(away != 0)
-    def _():
-        remote(s.wg4, s.wg4, s.wb_s.at[away - 1], s.wb_r.at[away - 1], (node_of(f, x, c), f)).wait_recv()
-
-    @pl.when(away == 0)
-    def _():
-        for d in range(1, zs):
-            to = (node_of(lax.rem(z + d, zs), x, c), f)
-            remote(s.wg4, s.wg4, s.wb_s.at[d - 1], s.wb_r.at[d - 1], to).wait_send()
-
-    s.wg5[c, x] = s.wg4[...]
-    last_copies = []
-    for i, (dx, dc) in enumerate(plane):
-        to = (node_of(z, lax.rem(x + dx, xs), lax.rem(c + dc, CORES)), f)
-        copy = remote(s.wg4, s.wg5.at[c, x], s.wl_s.at[i], s.wl_r.at[i], to)
-        copy.start()
-        last_copies.append(copy)
     for b in range(plan.blocks):
         out_ref[:, b * BLK : (b + 1) * BLK] = (s.bsum[idx[BL_END, b]] + s.rsum[idx[R_END, b]]).astype(BF16)
 
@@ -418,17 +420,25 @@
         "gp": vmem((plan.full, 2 * BLK), BF16),
         "gsend": vmem((ns, nf, 2, width, BLK), BF16),
         "grad": vmem((blocks + 1, width, BLK), BF16),
+        "send_sm": pltpu.SMEM((1, plan.nodes), jnp.int32),
+        "send_v": vmem((1, plan.nodes), jnp.int32),
+        "row_v": vmem((1, plan.tiles), jnp.int32),
+        "col_v": vmem((1, plan.tiles), jnp.int32),
+        "count_v": vmem((1, 1), jnp.int32),
+        "get_small": dma((5,)),
         "line": vmem((8, LANES), jnp.int32),
         "lists": vmem((LISTS, LANES), jnp.int32),
         "idx": pltpu.SMEM((LISTS, LANES), jnp.int32),
         "wg": vmem((CORES, nf, width, cols), F32),
-        "wg_c": vmem((nf, width, cols), F32),
+        "wg0": vmem((nf, width, cols), BF16),
+        "wg_c": vmem((nf, width, cols), BF16),
         "wg1": vmem((plan.xs - 1, nf, rows, cols), BF16),
         "wg_x": vmem((plan.xs - 1, nf, rows, cols), BF16),
         "wg2": vmem((nf, rows, cols), F32),
-        "wg_z": vmem((plan.zs - 1, rows, cols), F32),
-        "wg3": vmem((rows, cols), F32),
-        "wg_y": vmem((nf - 1, rows, cols), F32),
+        "wg2b": vmem((nf, rows, cols), BF16),
+        "wg_z": vmem((plan.zs, rows, cols), BF16),
+        "wg3": vmem((rows, cols), BF16),
+        "wg_y": vmem((nf - 1, rows, cols), BF16),
         "wg4": vmem((rows, cols), F32),
         "wg5": vmem((CORES, plan.xs, rows, cols), F32),
         "bsend": vmem((halo, width, BLK), BF16),
@@ -447,8 +457,7 @@
         "wc": dma((2,)),
         "wx_s": dma((plan.xs - 1,)), "wx_r": dma((plan.xs - 1,)),
         "wz_s": dma((plan.zs - 1,)), "wz_r": dma((plan.zs - 1,)),
-        "wy_s": dma((1,)), "wy_r": dma((nf - 1,)),
-        "wb_s": dma((plan.zs - 1,)), "wb_r": dma((plan.zs - 1,)),
+        "wy_s": dma((nf - 1,)), "wy_r": dma((nf - 1,)),
         "wl_s": dma((CORES * plan.xs - 1,)), "wl_r": dma((CORES * plan.xs - 1,)),
     }
 
@@ -460,7 +469,7 @@
     plan = Plan(blocks, width, tile_row.shape[0], feats, nodes, offsets_of(nodes), x_chips)
     scratch = scratch_of(plan)
     names = list(scratch)
-    given = 9
+    given = 8
 
     def body(*refs):
         s = Scratch()
@@ -470,22 +479,20 @@
 
     anywhere = pl.BlockSpec(memory_space=pltpu.HBM)
     in_vmem = pl.BlockSpec(memory_space=pltpu.VMEM)
-    in_smem = pl.BlockSpec(memory_space=pltpu.SMEM)
-    sends = send_blocks.reshape(1, nodes)
     grad_t, weight_sum = pl.pallas_call(
         body,
         out_shape=(
             pltpu.VMEM((width, rows_dev), BF16),
             pltpu.VMEM((width, plan.full), F32),
         ),
-        in_specs=[in_smem, in_smem, in_vmem, in_vmem, in_vmem, anywhere, anywhere, anywhere, anywhere],
+        in_specs=[anywhere] * given,
         out_specs=(in_vmem, in_vmem),
         scratch_shapes=[scratch[name] for name in names],
         compiler_params=pltpu.CompilerParams(
             collective_id=0, has_side_effects=True, vmem_limit_bytes=62 * 1024 * 1024
         ),
     )(
-        tile_count, sends, tile_row.reshape(1, -1), tile_col.reshape(1, -1), sends,
+        tile_count.reshape(1, 1), send_blocks.reshape(1, nodes), tile_row.reshape(1, -1), tile_col.reshape(1, -1),
         features.T, upstream.T, weight, tile_values,
     )
     return grad_t.T, weight_sum / math.sqrt(rows_dev * nodes)

time: 73.9 us -> 70.4 us (0.953)
  the two profiles are of different devices: /device:TPU:33 before, /device:TPU:1 now
where the time goes in v3:
time: 70.4 us; the launch traced here: 70.3 us
  Pallas kernels  67.5 us (96%)
  between operations  1.29 us (2%)
  local copies, waits for them, and re-layouts  0.8 us (1%)
    pallas_call x1, Pallas kernels, local(): pl.pallas_call(body, out_shape=(pltpu.VMEM((width, rows_dev), BF16), pltp...  67.5 us

profile of v3, /device:TPU:1, one launch (start us, length us, event | category | flops | bytes accessed | tf_op | source)
XLA Modules:
  0.0 70.3 jit_solution(12628508759284073454)
XLA Ops:
  1.3 67.5 %shard_map.95 = (bf16[64,4096]{1,0:T(8,128)(2,1)S(1)}, f32[64,512]{1,0:T(8,128)S(1)}) custom-call(s32[1,1]{1,0:T(1,128)} %bitcast.7.refs_0_, s32[1,64]{1,0:T(1,128)} %bitcast.11, s32[1,80]{1,0:T(1,128)} %bitcast.12, s32[1,80]{1,0:T(1,128)} %bitcast.13, bf16[64,4096]{1,0:T(8,128)(2,1)} %bitcast.9, bf16[64,4096]{1,0:T(8,128)(2,1)} %bitcast.10, ...), custom_call_target="tpu_custom_call" | custom-call | tf_op jit(solution)/shard_map/pallas_call | solution.py:482
  68.8 0.8 %copy.11 = bf16[4096,64]{0,1:T(8,128)(2,1)} copy(bf16[4096,64]{0,1:T(8,128)(2,1)S(1)} %bitcast.8) | data formatting | bytes 1048576
  69.6 0.7 broadcast_multiply_fusion

commit v4 on v3

--- a/solution.py
+++ b/solution.py
@@ -38,6 +38,7 @@
 MASK = (1 << BITS) - 1
 (FL_T, FL_C, FL_K, FL_END, FH_T, FH_S, FH_K, FH_END, BH_T, BH_R, BL_T, BL_R, BL_K, BL_END, R_S, R_K, R_END) = range(17)
 LISTS = 24
+HELD = 7
 
 
 def iota(dim, rows=LANES):
@@ -68,32 +69,50 @@
     return got & MASK, (got >> BITS) & MASK, got >> (2 * BITS), end
 
 
-def write_lists(plan, node, live, row_ref, col_ref, send_ref, line, lists):
+def write_order(plan, node, live, row_ref, col_ref, send_ref, line, first):
     n = plan.nodes
     lane = iota(1, 1)
     line[...] = jnp.zeros_like(line)
     line[0:1, 0 : plan.tiles] = row_ref[...]
     line[1:2, 0 : plan.tiles] = col_ref[...]
     line[2:3, 0:n] = send_ref[...]
-    row, col, sends = line[0:1, :], line[1:2, :], line[2:3, :]
+    row, col = line[0:1, :], line[1:2, :]
     alive = lane < live
-    local = jnp.logical_and(alive, col < plan.blocks)
-    row_in, col_in = jnp.where(local, row, plan.blocks), jnp.where(local, col, plan.blocks)
-    fl_t, fl_c, fl_k, fl_end = in_order(row_in, lane, col_in)
-    bl_t, bl_r, bl_k, bl_end = in_order(col_in, lane, row_in)
-
-    reads, serves = jnp.full((1, LANES), -1, jnp.int32), jnp.full((1, LANES), -1, jnp.int32)
+    reads = jnp.full((1, LANES), -1, jnp.int32)
     for i, d in enumerate(plan.offsets):
         reads = jnp.where(lane == i, plan.blocks + lax.rem(node + d + n, n), reads)
-        serves = jnp.where(lane == i, lax.rem(node - d + n, n), serves)
     packed = as_columns(jnp.where(alive, col + (row << BITS), 0))
     got = pick((packed & MASK) == reads, (packed >> BITS) + (iota(0) << BITS))
     bh_t, bh_r = got >> BITS, got & MASK
+    rows_used = as_columns(jnp.where(lane < plan.halo, bh_r, plan.blocks))
+    group = jnp.where(lane < plan.blocks, jnp.where(count(rows_used == lane) > 0, 0, 1), 2)
+    down = as_columns(group)
+    place = count(down < group) + count(jnp.logical_and(down == group, iota(0) < iota(1)))
+    place_down = as_columns(place)
+    order = pick(place_down == lane, iota(0))
+    first[...] = jnp.zeros_like(first)
+    first[0:1, :] = order
+    return bh_t, bh_r, place_down
+
+
+def write_lists(plan, node, live, order, line, lists):
+    n = plan.nodes
+    lane = iota(1, 1)
+    bh_t, bh_r, place_down = order
+    row, col, sends = line[0:1, :], line[1:2, :], line[2:3, :]
+    local = jnp.logical_and(lane < live, col < plan.blocks)
+    row_in, col_in = jnp.where(local, row, plan.blocks), jnp.where(local, col, plan.blocks)
+    fl_t, fl_c, fl_k, fl_end = in_order(row_in, lane, col_in)
+    bl_t, bl_r, bl_k, bl_end = in_order(col_in, lane, pick(iota(0) == row_in, place_down))
+    serves = jnp.full((1, LANES), -1, jnp.int32)
+    for i, d in enumerate(plan.offsets):
+        serves = jnp.where(lane == i, lax.rem(node - d + n, n), serves)
     target = pick(iota(0) == serves, as_columns(sends))
     used = lane < plan.halo
     fh_t, fh_s, fh_k, fh_end = in_order(jnp.where(used, bh_r, plan.blocks), bh_t, lane)
     r_s, _, r_k, r_end = in_order(jnp.where(used, target, plan.blocks), lane, lane)
-    rows = [fl_t, fl_c, fl_k, fl_end, fh_t, fh_s, fh_k, fh_end, bh_t, bh_r, bl_t, bl_r, bl_k, bl_end, r_s, r_k, r_end]
+    bh_p = pick(iota(0) == bh_r, place_down)
+    rows = [fl_t, fl_c, fl_k, fl_end, fh_t, fh_s, fh_k, fh_end, bh_t, bh_p, bl_t, bl_r, bl_k, bl_end, r_s, r_k, r_end]
     lists[...] = jnp.zeros_like(lists)
     for i, vector in enumerate(rows):
         lists[i : i + 1, :] = vector
@@ -118,15 +137,12 @@
             src_ref=src, dst_ref=dst, send_sem=send_sem, recv_sem=recv_sem, device_id=to, device_id_type=MESH
         )
 
-    def up_pair(p):
-        return up_hbm.at[:, pl.ds(pl.multiple_of(p * pair, pair), pair)]
-
     get_feats = pltpu.make_async_copy(feats_hbm, s.feats, s.get.at[0])
     get_w = pltpu.make_async_copy(
         w_hbm.at[pl.ds(x * rows, rows), pl.ds(pl.multiple_of(c * cols, cols), cols)], s.wq.at[c, x, f], s.get.at[1]
     )
     get_tiles = pltpu.make_async_copy(tiles_hbm, s.tiles, s.get.at[2])
-    get_up = [pltpu.make_async_copy(up_pair(k * nf + f), s.ur.at[k, f], s.get.at[3 + k]) for k in range(plan.stages)]
+    get_up = pltpu.make_async_copy(up_hbm, s.up, s.get.at[3])
     get_send = pltpu.make_async_copy(send_hbm, s.send_sm, s.get_small.at[0])
     get_lines = [
         pltpu.make_async_copy(src, dst, s.get_small.at[1 + i])
@@ -134,7 +150,7 @@
             [(send_hbm, s.send_v), (row_hbm, s.row_v), (col_hbm, s.col_v), (count_hbm, s.count_v)]
         )
     ]
-    for copy in [get_w, get_send, get_feats, get_tiles] + get_up + get_lines:
+    for copy in [get_w, get_send] + get_lines + [get_feats, get_up, get_tiles]:
         copy.start()
 
     near = sorted({d % nn for d in plan.offsets} | {-d % nn for d in plan.offsets})
@@ -155,17 +171,16 @@
         remote(s.wq.at[c, x, f], s.wq.at[c, x, f], s.w_s.at[d - 1], s.w_r.at[d - 1], (node, lax.rem(f + d, nf)))
         for d in far_first
     ]
-    up_copies = []
-    for k in range(plan.stages):
-        stage_copies = []
-        for d in far_first:
-            j = lax.rem(f + d, nf)
-            stage_copies.append(
-                remote(up_pair(k * nf + j), s.ur.at[k, f], s.up_s.at[k, d - 1], s.up_r.at[k, d - 1], (node, j))
-            )
-        up_copies.append(stage_copies)
-    for copy in w_copies + up_copies[0]:
-        copy.start()
+    for copy in w_copies:
+        copy.start()
+
+    for copy in get_lines:
+        copy.wait()
+    live = s.count_v[...]
+    order = write_order(plan, node, live, s.row_v, s.col_v, s.send_v, s.line, s.order_v)
+    put_order = pltpu.make_async_copy(s.order_v, s.order, s.get.at[4])
+    put_order.start()
+
     get_feats.wait()
     get_send.wait()
     for b in range(plan.blocks):
@@ -178,13 +193,28 @@
         copy = remote(s.hsend.at[i], s.hrecv.at[i], s.halo_s.at[i], s.halo_r.at[i], (to, f))
         copy.start()
         halo_copies.append(copy)
-    for copy in sum(up_copies[1:], []):
-        copy.start()
-
-    for copy in get_lines:
-        copy.wait()
-    write_lists(plan, node, s.count_v[...], s.row_v, s.col_v, s.send_v, s.line, s.lists)
-    put_lists = pltpu.make_async_copy(s.lists, s.idx, s.get.at[3 + plan.stages])
+
+    get_up.wait()
+    for b in range(plan.blocks):
+        s.uptable[b] = s.up[:, b * BLK : (b + 1) * BLK]
+    put_order.wait()
+    up_copies = []
+    for k in range(plan.stages):
+        stage_copies = []
+        for d in far_first + [0]:
+            j = lax.rem(f + d, nf)
+            p = k * nf + j
+            into = s.upk.at[p] if d else s.ur.at[k, f]
+            into[:, 0:BLK] = s.uptable[s.order[0, 2 * p]]
+            into[:, BLK:pair] = s.uptable[s.order[0, 2 * p + 1]]
+            if d:
+                copy = remote(s.upk.at[p], s.ur.at[k, f], s.up_s.at[k, d - 1], s.up_r.at[k, d - 1], (node, j))
+                copy.start()
+                stage_copies.append(copy)
+        up_copies.append(stage_copies)
+
+    write_lists(plan, node, live, order, s.line, s.lists)
+    put_lists = pltpu.make_async_copy(s.lists, s.idx, s.get.at[5])
     put_lists.start()
     zero = jnp.zeros((width, BLK), F32)
     for ref in (s.fsum, s.hsum, s.bsum, s.rsum):
@@ -228,7 +258,8 @@
 
     lax.fori_loop(0, plan.halo, forward_halo, zero, unroll=plan.halo)
 
-    def summed(b):
+    def summed(at):
+        b = s.order[0, at]
         return (s.fsum[idx[FL_END, b]] + s.hsum[idx[FH_END, b]]).astype(BF16)
 
     agg_copies = []
@@ -258,39 +289,35 @@
                 s.wfull[pl.ds(j * width + at * rows, rows), pl.ds(h * cols, cols)] = s.wq[h, at, j]
     s.wt[...] = s.wfull[...].T
 
-    grad_copies = []
-
-    def send_grad(k):
-        for d in far_first:
+    grad_copies = [[] for _ in range(plan.stages)]
+
+    def send_grad(k, distances):
+        for d in distances:
             j = lax.rem(f + d, nf)
-            copy = remote(
-                s.gsend.at[k, j], s.grad.at[pl.ds(2 * (k * nf + f), 2)], s.gr_s.at[k, d - 1], s.gr_r.at[k, d - 1], (node, j)
-            )
+            into = s.first.at[pl.ds(2 * f, 2)] if k == 0 else s.grad.at[pl.ds(2 * (k * nf + f), 2)]
+            copy = remote(s.gsend.at[k, j], into, s.gr_s.at[k, d - 1], s.gr_r.at[k, d - 1], (node, j))
             copy.start()
-            grad_copies.append(copy)
+            grad_copies[k].append(copy)
 
     for k in range(plan.stages):
-        get_up[k].wait()
         for copy in up_copies[k] + agg_copies[k]:
             copy.wait()
         if k:
-            send_grad(k - 1)
+            send_grad(k - 1, far_first)
         agg = s.ar[k].reshape(plan.full, pair)
         pre = jnp.dot(s.wt[...], agg, preferred_element_type=F32)
         sig = jax.nn.sigmoid(pre)
         upstream = s.ur[k].reshape(plan.full, pair).astype(F32)
         s.gp[...] = (upstream * sig * (1.0 + pre * (1.0 - sig))).astype(BF16)
 
-        def weight_part():
-            wg = lax.dot_general(agg, s.gp[...], (((1,), (1,)), ((), ())), preferred_element_type=F32)
-            for h in range(CORES):
-                part = wg[:, h * cols : (h + 1) * cols].reshape(nf, width, cols)
-                s.wg[h] = part if k == 0 else s.wg[h] + part
+        def weight_part(h):
+            columns = s.gp[pl.ds(pl.multiple_of(h * cols, cols), cols)]
+            wg = lax.dot_general(agg, columns, (((1,), (1,)), ((), ())), preferred_element_type=F32)
+            return wg.reshape(nf, width, cols) + (s.wg[h] if k else 0.0)
 
         last = k == plan.stages - 1
         if last:
-            weight_part()
-            s.wg0[...] = s.wg[1 - c].astype(BF16)
+            s.wg0[...] = weight_part(1 - c).astype(BF16)
             wg_core = remote(s.wg0, s.wg_c, s.wc.at[0], s.wc.at[1], other)
             wg_core.start()
         grad = jnp.dot(s.wfull[...], s.gp[...], preferred_element_type=F32).astype(BF16)
@@ -298,10 +325,14 @@
             for h in range(2):
                 s.gsend[k, j, h] = grad[j * width : (j + 1) * width, h * BLK : (h + 1) * BLK]
         if last:
-            send_grad(k)
-        s.grad[pl.ds(2 * (k * nf + f), 2)] = s.gsend[k, f]
-        if not last:
-            weight_part()
+            send_grad(k, far_first[HELD:])
+        into = s.first.at[pl.ds(2 * f, 2)] if k == 0 else s.grad.at[pl.ds(2 * (k * nf + f), 2)]
+        into[...] = s.gsend[k, f]
+        if last:
+            s.wg[c] = weight_part(c)
+        else:
+            for h in range(CORES):
+                s.wg[h] = weight_part(h)
 
     wg_core.wait()
     x_copies = []
@@ -327,6 +358,20 @@
         copy = remote(s.wg2b.at[j], s.wg_y.at[d - 1], s.wy_s.at[d - 1], s.wy_r.at[d - 1], (node, j))
         copy.start()
         y_copies.append(copy)
+    send_grad(plan.stages - 1, far_first[:HELD])
+    for copy in grad_copies[0]:
+        copy.wait()
+    back_copies = []
+    for i, d in enumerate(plan.offsets):
+        term = jnp.dot(s.first[idx[BH_R, i]], s.tiles[idx[BH_T, i]], preferred_element_type=F32)
+        s.bsend[i] = term.astype(BF16)
+        copy = remote(
+            s.bsend.at[i], s.brecv.at[i], s.back_s.at[i], s.back_r.at[i], (lax.rem(node + d + nn, nn), f)
+        )
+        copy.start()
+        back_copies.append(copy)
+    s.grad[pl.ds(0, 2 * nf)] = s.first[...]
+
     for copy in y_copies:
         copy.wait()
     s.wg3[...] = sum([s.wg_y[d].astype(F32) for d in range(nf - 1)], s.wg2[f]).astype(BF16)
@@ -338,17 +383,19 @@
         copy.start()
         z_copies.append(copy)
 
-    for copy in grad_copies:
-        copy.wait()
-    back_copies = []
-    for i, d in enumerate(plan.offsets):
-        term = jnp.dot(s.grad[idx[BH_R, i]], s.tiles[idx[BH_T, i]], preferred_element_type=F32)
-        s.bsend[i] = term.astype(BF16)
-        copy = remote(
-            s.bsend.at[i], s.brecv.at[i], s.back_s.at[i], s.back_r.at[i], (lax.rem(node + d + nn, nn), f)
-        )
-        copy.start()
-        back_copies.append(copy)
+    for copy in z_copies:
+        copy.wait()
+    s.wg4[...] = sum([s.wg_z[at].astype(F32) for at in range(1, zs)], s.wg_z[0].astype(F32))
+    s.wg5[c, x] = s.wg4[...]
+    last_copies = []
+    for i, (dx, dc) in enumerate(plane):
+        to = (node_of(z, lax.rem(x + dx, xs), lax.rem(c + dc, CORES)), f)
+        copy = remote(s.wg4, s.wg5.at[c, x], s.wl_s.at[i], s.wl_r.at[i], to)
+        copy.start()
+        last_copies.append(copy)
+
+    for copy in sum(grad_copies[1:], []):
+        copy.wait()
 
     def backward_local(i, total):
         keep = idx[BL_K, i].astype(F32)
@@ -357,21 +404,7 @@
         s.bsum[i + 1] = total
         return total
 
-    middle = plan.local // 2
-    total = lax.fori_loop(0, middle, backward_local, zero, unroll=16)
-
-    for copy in z_copies:
-        copy.wait()
-    s.wg4[...] = sum([s.wg_z[at].astype(F32) for at in range(1, zs)], s.wg_z[0].astype(F32))
-    s.wg5[c, x] = s.wg4[...]
-    last_copies = []
-    for i, (dx, dc) in enumerate(plane):
-        to = (node_of(z, lax.rem(x + dx, xs), lax.rem(c + dc, CORES)), f)
-        copy = remote(s.wg4, s.wg5.at[c, x], s.wl_s.at[i], s.wl_r.at[i], to)
-        copy.start()
-        last_copies.append(copy)
-
-    lax.fori_loop(middle, plan.local, backward_local, total, unroll=16)
+    lax.fori_loop(0, plan.local, backward_local, zero, unroll=16)
 
     for copy in back_copies:
         copy.wait()
@@ -406,6 +439,9 @@
     return {
         "feats": vmem((width, blocks * BLK), BF16),
         "table": vmem((blocks + 1, width, BLK), BF16),
+        "up": vmem((width, blocks * BLK), BF16),
+        "uptable": vmem((blocks, width, BLK), BF16),
+        "upk": vmem((blocks // 2, width, 2 * BLK), BF16),
         "ur": vmem((ns, nf, width, 2 * BLK), BF16),
         "wq": vmem((CORES, plan.xs, nf, rows, cols), BF16),
         "wfull": vmem((plan.full, plan.full), BF16),
@@ -419,6 +455,7 @@
         "ar": vmem((ns, nf, width, 2 * BLK), BF16),
         "gp": vmem((plan.full, 2 * BLK), BF16),
         "gsend": vmem((ns, nf, 2, width, BLK), BF16),
+        "first": vmem((2 * nf, width, BLK), BF16),
         "grad": vmem((blocks + 1, width, BLK), BF16),
         "send_sm": pltpu.SMEM((1, plan.nodes), jnp.int32),
         "send_v": vmem((1, plan.nodes), jnp.int32),
@@ -427,6 +464,8 @@
         "count_v": vmem((1, 1), jnp.int32),
         "get_small": dma((5,)),
         "line": vmem((8, LANES), jnp.int32),
+        "order_v": vmem((8, LANES), jnp.int32),
+        "order": pltpu.SMEM((8, LANES), jnp.int32),
         "lists": vmem((LISTS, LANES), jnp.int32),
         "idx": pltpu.SMEM((LISTS, LANES), jnp.int32),
         "wg": vmem((CORES, nf, width, cols), F32),
@@ -445,7 +484,7 @@
         "brecv": vmem((halo, width, BLK), BF16),
         "bsum": vmem((plan.local + 1, width, BLK), F32),
         "rsum": vmem((halo + 1, width, BLK), F32),
-        "get": dma((4 + ns,)),
+        "get": dma((6,)),
         "halo_s": dma((halo,)), "halo_r": dma((halo,)),
         "w_s": dma((nf - 1,)), "w_r": dma((nf - 1,)),
         "wqx_s": dma((plan.xs - 1,)), "wqx_r": dma((plan.xs - 1,)),

time: 70.4 us -> 67.8 us (0.963)
  Pallas kernels: 67.5 us -> 65 us
    pallas_call x1, Pallas kernels: 67.5 us -> 65 us  [local(): pl.pallas_call(body, out_shape=(pltpu.VMEM((width, rows_dev), BF16), pltp...]
where the time goes in v4:
time: 67.8 us; the launch traced here: 67.7 us
  Pallas kernels  65 us (96%)
  between operations  1.29 us (2%)
  local copies, waits for them, and re-layouts  0.8 us (1%)
    pallas_call x1, Pallas kernels, local(): pl.pallas_call(body, out_shape=(pltpu.VMEM((width, rows_dev), BF16), pltp...  65 us

profile of v4, /device:TPU:1, one launch (start us, length us, event | category | flops | bytes accessed | tf_op | source)
XLA Modules:
  0.0 67.7 jit_solution(5551763965383197789)
XLA Ops:
  1.3 65.0 %shard_map.95 = (bf16[64,4096]{1,0:T(8,128)(2,1)S(1)}, f32[64,512]{1,0:T(8,128)S(1)}) custom-call(s32[1,1]{1,0:T(1,128)} %bitcast.7.refs_0_, s32[1,64]{1,0:T(1,128)} %bitcast.11, s32[1,80]{1,0:T(1,128)} %bitcast.12, s32[1,80]{1,0:T(1,128)} %bitcast.13, bf16[64,4096]{1,0:T(8,128)(2,1)} %bitcast.9, bf16[64,4096]{1,0:T(8,128)(2,1)} %bitcast.10, ...), custom_call_target="tpu_custom_call" | custom-call | tf_op jit(solution)/shard_map/pallas_call | solution.py:521
  66.2 0.8 %copy.11 = bf16[4096,64]{0,1:T(8,128)(2,1)} copy(bf16[4096,64]{0,1:T(8,128)(2,1)S(1)} %bitcast.8) | data formatting | bytes 1048576
  67.0 0.7 broadcast_multiply_fusion

commit v5 on v4

--- a/solution.py
+++ b/solution.py
@@ -38,7 +38,7 @@
 MASK = (1 << BITS) - 1
 (FL_T, FL_C, FL_K, FL_END, FH_T, FH_S, FH_K, FH_END, BH_T, BH_R, BL_T, BL_R, BL_K, BL_END, R_S, R_K, R_END) = range(17)
 LISTS = 24
-HELD = 7
+HELD = 5
 
 
 def iota(dim, rows=LANES):
@@ -137,6 +137,18 @@
             src_ref=src, dst_ref=dst, send_sem=send_sem, recv_sem=recv_sem, device_id=to, device_id_type=MESH
         )
 
+    near = sorted({d % nn for d in plan.offsets} | {-d % nn for d in plan.offsets})
+    z_far_first = sorted(range(1, zs), key=lambda d: -min(d, zs - d))
+    x_far_first = sorted(range(1, xs), key=lambda d: -min(d, xs - d))
+    plane = [(dx, dc) for dx in x_far_first for dc in range(CORES)] + [(0, 1)]
+    partners = [(node_of(lax.rem(z + d, zs), x, c), f) for d in z_far_first if d * xs * CORES not in near]
+    partners += [(lax.rem(node + d, nn), f) for d in near]
+    partners += [(node_of(z, lax.rem(x + dx, xs), lax.rem(c + dc, CORES)), f) for dx, dc in plane]
+    partners += [(node, lax.rem(f + d, nf)) for d in range(1, nf)]
+    barrier = pltpu.get_barrier_semaphore()
+    for to in partners:
+        pl.semaphore_signal(barrier, inc=1, device_id=to, device_id_type=MESH)
+
     get_feats = pltpu.make_async_copy(feats_hbm, s.feats, s.get.at[0])
     get_w = pltpu.make_async_copy(
         w_hbm.at[pl.ds(x * rows, rows), pl.ds(pl.multiple_of(c * cols, cols), cols)], s.wq.at[c, x, f], s.get.at[1]
@@ -150,19 +162,19 @@
             [(send_hbm, s.send_v), (row_hbm, s.row_v), (col_hbm, s.col_v), (count_hbm, s.count_v)]
         )
     ]
-    for copy in [get_w, get_send] + get_lines + [get_feats, get_up, get_tiles]:
-        copy.start()
-
-    near = sorted({d % nn for d in plan.offsets} | {-d % nn for d in plan.offsets})
-    plane = [(dx, dc) for dx in range(xs) for dc in range(CORES) if dx or dc]
-    partners = [(node_of(lax.rem(z + d, zs), x, c), f) for d in range(1, zs)]
-    partners += [(lax.rem(node + d, nn), f) for d in near]
-    partners += [(node_of(z, lax.rem(x + dx, xs), lax.rem(c + dc, CORES)), f) for dx, dc in plane]
-    partners += [(node, lax.rem(f + d, nf)) for d in range(1, nf)]
-    barrier = pltpu.get_barrier_semaphore()
-    for to in partners:
-        pl.semaphore_signal(barrier, inc=1, device_id=to, device_id_type=MESH)
-
+    for copy in get_lines + [get_up, get_w, get_send, get_feats, get_tiles]:
+        copy.start()
+
+    for copy in get_lines:
+        copy.wait()
+    live = s.count_v[...]
+    order = write_order(plan, node, live, s.row_v, s.col_v, s.send_v, s.line, s.order_v)
+    put_order = pltpu.make_async_copy(s.order_v, s.order, s.get.at[4])
+    put_order.start()
+
+    get_up.wait()
+    for b in range(plan.blocks):
+        s.uptable[b] = s.up[:, b * BLK : (b + 1) * BLK]
     get_w.wait()
     pl.semaphore_wait(barrier, len(partners))
 
@@ -174,32 +186,10 @@
     for copy in w_copies:
         copy.start()
 
-    for copy in get_lines:
-        copy.wait()
-    live = s.count_v[...]
-    order = write_order(plan, node, live, s.row_v, s.col_v, s.send_v, s.line, s.order_v)
-    put_order = pltpu.make_async_copy(s.order_v, s.order, s.get.at[4])
-    put_order.start()
-
-    get_feats.wait()
-    get_send.wait()
-    for b in range(plan.blocks):
-        s.table[b] = s.feats[:, b * BLK : (b + 1) * BLK]
-    s.table[plan.blocks] = jnp.zeros((width, BLK), BF16)
-    halo_copies = []
-    for i, d in enumerate(plan.offsets):
-        to = lax.rem(node - d + nn, nn)
-        s.hsend[i] = s.table[s.send_sm[0, to]]
-        copy = remote(s.hsend.at[i], s.hrecv.at[i], s.halo_s.at[i], s.halo_r.at[i], (to, f))
-        copy.start()
-        halo_copies.append(copy)
-
-    get_up.wait()
-    for b in range(plan.blocks):
-        s.uptable[b] = s.up[:, b * BLK : (b + 1) * BLK]
     put_order.wait()
     up_copies = []
-    for k in range(plan.stages):
+
+    def send_up(k):
         stage_copies = []
         for d in far_first + [0]:
             j = lax.rem(f + d, nf)
@@ -213,6 +203,23 @@
                 stage_copies.append(copy)
         up_copies.append(stage_copies)
 
+    send_up(0)
+    get_feats.wait()
+    get_send.wait()
+    for b in range(plan.blocks):
+        s.table[b] = s.feats[:, b * BLK : (b + 1) * BLK]
+    s.table[plan.blocks] = jnp.zeros((width, BLK), BF16)
+    halo_copies = []
+    for i, d in enumerate(plan.offsets):
+        to = lax.rem(node - d + nn, nn)
+        s.hsend[i] = s.table[s.send_sm[0, to]]
+        copy = remote(s.hsend.at[i], s.hrecv.at[i], s.halo_s.at[i], s.halo_r.at[i], (to, f))
+        copy.start()
+        halo_copies.append(copy)
+
+    for k in range(1, plan.stages):
+        send_up(k)
+
     write_lists(plan, node, live, order, s.line, s.lists)
     put_lists = pltpu.make_async_copy(s.lists, s.idx, s.get.at[5])
     put_lists.start()
@@ -224,7 +231,7 @@
     for copy in w_copies:
         copy.wait()
     wx_copies = []
-    for d in range(1, xs):
+    for d in x_far_first:
         to = (node_of(z, lax.rem(x + d, xs), c), f)
         wx_copies.append(remote(s.wq.at[c, x], s.wq.at[c, x], s.wqx_s.at[d - 1], s.wqx_r.at[d - 1], to))
     for copy in wx_copies:
@@ -336,7 +343,7 @@
 
     wg_core.wait()
     x_copies = []
-    for d in list(range(1, xs)) + [0]:
+    for d in x_far_first + [0]:
         to_x = lax.rem(x + d, xs)
         at = pl.ds(pl.multiple_of(to_x * rows, rows), rows)
         part = s.wg[c, :, at, :] + s.wg_c[:, at, :].astype(F32)
@@ -377,7 +384,7 @@
     s.wg3[...] = sum([s.wg_y[d].astype(F32) for d in range(nf - 1)], s.wg2[f]).astype(BF16)
     s.wg_z[z] = s.wg3[...]
     z_copies = []
-    for d in range(1, zs):
+    for d in z_far_first:
         to = (node_of(lax.rem(z + d, zs), x, c), f)
         copy = remote(s.wg3, s.wg_z.at[z], s.wz_s.at[d - 1], s.wz_r.at[d - 1], to)
         copy.start()

time: 67.8 us -> 67.4 us (level)
  no operation moved by 1% of the time
where the time goes in v5:
time: 67.4 us; the launch traced here: 67.3 us
  Pallas kernels  64.5 us (96%)
  between operations  1.29 us (2%)
  local copies, waits for them, and re-layouts  0.8 us (1%)
    pallas_call x1, Pallas kernels, local(): pl.pallas_call(body, out_shape=(pltpu.VMEM((width, rows_dev), BF16), pltp...  64.5 us

profile of v5, /device:TPU:1, one launch (start us, length us, event | category | flops | bytes accessed | tf_op | source)
XLA Modules:
  0.0 67.3 jit_solution(14644086196473105899)
XLA Ops:
  1.3 64.5 %shard_map.95 = (bf16[64,4096]{1,0:T(8,128)(2,1)S(1)}, f32[64,512]{1,0:T(8,128)S(1)}) custom-call(s32[1,1]{1,0:T(1,128)} %bitcast.7.refs_0_, s32[1,64]{1,0:T(1,128)} %bitcast.11, s32[1,80]{1,0:T(1,128)} %bitcast.12, s32[1,80]{1,0:T(1,128)} %bitcast.13, bf16[64,4096]{1,0:T(8,128)(2,1)} %bitcast.9, bf16[64,4096]{1,0:T(8,128)(2,1)} %bitcast.10, ...), custom_call_target="tpu_custom_call" | custom-call | tf_op jit(solution)/shard_map/pallas_call | solution.py:528
  65.8 0.8 %copy.11 = bf16[4096,64]{0,1:T(8,128)(2,1)} copy(bf16[4096,64]{0,1:T(8,128)(2,1)S(1)} %bitcast.8) | data formatting | bytes 1048576
  66.6 0.7 broadcast_multiply_fusion

commit v6 on v5

--- a/solution.py
+++ b/solution.py
@@ -38,7 +38,7 @@
 MASK = (1 << BITS) - 1
 (FL_T, FL_C, FL_K, FL_END, FH_T, FH_S, FH_K, FH_END, BH_T, BH_R, BL_T, BL_R, BL_K, BL_END, R_S, R_K, R_END) = range(17)
 LISTS = 24
-HELD = 5
+HELD = 7
 
 
 def iota(dim, rows=LANES):
@@ -356,7 +356,7 @@
         else:
             s.wg2[...] = part
     for copy in x_copies:
-        copy.wait()
+        copy.wait_recv()
     s.wg2[...] = sum([s.wg_x[d].astype(F32) for d in range(xs - 1)], s.wg2[...])
     s.wg2b[...] = s.wg2[...].astype(BF16)
     y_copies = []
@@ -380,7 +380,7 @@
     s.grad[pl.ds(0, 2 * nf)] = s.first[...]
 
     for copy in y_copies:
-        copy.wait()
+        copy.wait_recv()
     s.wg3[...] = sum([s.wg_y[d].astype(F32) for d in range(nf - 1)], s.wg2[f]).astype(BF16)
     s.wg_z[z] = s.wg3[...]
     z_copies = []
@@ -391,7 +391,7 @@
         z_copies.append(copy)
 
     for copy in z_copies:
-        copy.wait()
+        copy.wait_recv()
     s.wg4[...] = sum([s.wg_z[at].astype(F32) for at in range(1, zs)], s.wg_z[0].astype(F32))
     s.wg5[c, x] = s.wg4[...]
     last_copies = []
@@ -427,6 +427,8 @@
     for b in range(plan.blocks):
         out_ref[:, b * BLK : (b + 1) * BLK] = (s.bsum[idx[BL_END, b]] + s.rsum[idx[R_END, b]]).astype(BF16)
 
+    for copy in x_copies + y_copies + z_copies:
+        copy.wait_send()
     for copy in last_copies:
         copy.wait()
     for h in range(CORES):

time: 67.4 us -> 67.1 us (level)
  no operation moved by 1% of the time
where the time goes in v6:
time: 67.1 us; the launch traced here: 66.9 us
  Pallas kernels  64.2 us (96%)
  between operations  1.29 us (2%)
  local copies, waits for them, and re-layouts  0.8 us (1%)
    pallas_call x1, Pallas kernels, local(): pl.pallas_call(body, out_shape=(pltpu.VMEM((width, rows_dev), BF16), pltp...  64.2 us

profile of v6, /device:TPU:1, one launch (start us, length us, event | category | flops | bytes accessed | tf_op | source)
XLA Modules:
  0.0 66.9 jit_solution(8274773580249005451)
XLA Ops:
  1.3 64.2 %shard_map.95 = (bf16[64,4096]{1,0:T(8,128)(2,1)S(1)}, f32[64,512]{1,0:T(8,128)S(1)}) custom-call(s32[1,1]{1,0:T(1,128)} %bitcast.7.refs_0_, s32[1,64]{1,0:T(1,128)} %bitcast.11, s32[1,80]{1,0:T(1,128)} %bitcast.12, s32[1,80]{1,0:T(1,128)} %bitcast.13, bf16[64,4096]{1,0:T(8,128)(2,1)} %bitcast.9, bf16[64,4096]{1,0:T(8,128)(2,1)} %bitcast.10, ...), custom_call_target="tpu_custom_call" | custom-call | tf_op jit(solution)/shard_map/pallas_call | solution.py:530
  65.5 0.8 %copy.11 = bf16[4096,64]{0,1:T(8,128)(2,1)} copy(bf16[4096,64]{0,1:T(8,128)(2,1)S(1)} %bitcast.8) | data formatting | bytes 1048576
  66.3 0.7 broadcast_multiply_fusion
